TPU v7x, 128 devices: a whole 4x4x4 slice. The times are simulated.
128 devices in a mesh: section: 4 (over z), row: 8 (over x, core), col: 4 (over y).
Axes of the slice: x: 4, y: 4, z: 4, core: 2. Of those that a mesh axis runs over, the one named last changes fastest.
Arguments:
- hidden: bfloat16 [4, 64, 5120], P('section', None, ('row', 'col')), may hold values from -64 to 64
- lengths: int32 [4, 64], P(None, 'row'), may hold values from 24 to 96, as said below
- attn_gain: bfloat16 [4, 5120], P('section', ('row', 'col')), may hold values from 0.099609375 to 1.8984375
- ffn_gain: bfloat16 [4, 5120], P('section', ('row', 'col')), may hold values from 0.099609375 to 1.8984375
- q_weight: bfloat16 [4, 5120, 5120], P('section', 'row', 'col'), may hold values from -0.078125 to 0.078125
- key_weight: bfloat16 [4, 5120, 1024], P('section', 'row', 'col'), may hold values from -0.078125 to 0.078125
- value_weight: bfloat16 [4, 5120, 1024], P('section', 'row', 'col'), may hold values from -0.078125 to 0.078125
- out_weight: bfloat16 [4, 5120, 5120], P('section', 'col', 'row'), may hold values from -0.125 to 0.125
- gate_weight: bfloat16 [4, 5120, 16384], P('section', None, ('row', 'col')), may hold values from -0.078125 to 0.078125
- up_weight: bfloat16 [4, 5120, 16384], P('section', None, ('row', 'col')), may hold values from -0.078125 to 0.078125
- down_weight: bfloat16 [4, 16384, 5120], P('section', ('row', 'col')), may hold values from -0.09375 to 0.09375
- key_cache: bfloat16 [4, 4, 64, 8, 96, 128], P('section', None, 'row', 'col'), may hold values from -256 to 256
- value_cache: bfloat16 [4, 4, 64, 8, 96, 128], P('section', None, 'row', 'col'), may hold values from -6 to 6
Outputs:
- states: bfloat16 [4, 64, 5120], P('section', None, ('row', 'col'))
Inputs may be any that keep to these rules, and one draw needn't show every extreme that they name: `lengths`: in every micro-batch one stream has exactly 96 cached positions and another exactly 24.
All inputs are finite; a program needn't handle non-finite values.
Results may differ from a plain program's by a relative error of at most 0.035.
Values may be sent and summed in bfloat16 or wider, within the bound.
A program may use at most 128 MiB of HBM per device.

v0:
```python
import math

import jax
import jax.numpy as jnp
from jax import lax
from jax.sharding import PartitionSpec as P

D = 5120
HD = 128


norm_eps = 1e-06
masked_score = -1e30


def shifted(value, axis, steps):
    count = lax.axis_size(axis)
    pairs = [(source, (source + steps) % count) for source in range(count)]
    return lax.ppermute(value, axis, pairs)


def product(left, right):
    return jnp.dot(left, right, preferred_element_type=jnp.float32)


def attention(queries, new_keys, new_values, cached_keys, cached_values, live_lengths):
    streams = queries.shape[0]
    groups = cached_keys.shape[1]
    per_group = queries.shape[1] // (groups * HD)
    query_tiles = queries.reshape(streams, groups, per_group, HD)
    key_new = new_keys.reshape(streams, groups, HD)
    value_new = new_values.reshape(streams, groups, HD)
    score_scale = 1.0 / math.sqrt(HD)
    scores = (
        jnp.einsum("bgqd,bgtd->bgqt", query_tiles, cached_keys, preferred_element_type=jnp.float32)
        * score_scale
    )
    self_score = (
        jnp.einsum("bgqd,bgd->bgq", query_tiles, key_new, preferred_element_type=jnp.float32)
        * score_scale
    )
    positions = lax.broadcasted_iota(jnp.int32, (streams, cached_keys.shape[2]), 1)
    valid = positions < live_lengths[:, None]
    scores = jnp.where(valid[:, None, None, :], scores, masked_score)
    row_max = jnp.maximum(jnp.max(scores, axis=-1), self_score)
    weights = jnp.exp(scores - row_max[..., None])
    self_weight = jnp.exp(self_score - row_max)
    denominator = jnp.sum(weights, axis=-1) + self_weight
    probs = (weights / denominator[..., None]).astype(jnp.bfloat16)
    self_prob = (self_weight / denominator).astype(jnp.bfloat16)
    mixed = jnp.einsum("bgqt,bgtd->bgqd", probs, cached_values, preferred_element_type=jnp.float32)
    mixed = (
        mixed
        + self_prob.astype(jnp.float32)[..., None] * value_new.astype(jnp.float32)[:, :, None, :]
    )
    return mixed.reshape(streams, groups * per_group * HD).astype(jnp.bfloat16)


def per_device(
    hidden,
    lengths,
    attn_gain,
    ffn_gain,
    q_weight,
    key_weight,
    value_weight,
    out_weight,
    gate_weight,
    up_weight,
    down_weight,
    key_cache,
    value_cache,
):
    section_count = lax.axis_size("section")
    section_here = lax.axis_index("section")
    current = hidden[0]
    local_streams = lengths.shape[1]
    gain_first = attn_gain[0]
    gain_second = ffn_gain[0]
    query_proj = q_weight[0]
    key_proj = key_weight[0]
    value_proj = value_weight[0]
    output_proj = out_weight[0]
    gate_proj = gate_weight[0]
    up_proj = up_weight[0]
    down_proj = down_weight[0]
    for step_index in range(section_count):
        micro_batch = (section_here - step_index) % section_count
        live_lengths = lax.dynamic_index_in_dim(lengths, micro_batch, 0, keepdims=False)
        cached_keys = lax.dynamic_index_in_dim(key_cache[0], micro_batch, 0, keepdims=False)
        cached_values = lax.dynamic_index_in_dim(value_cache[0], micro_batch, 0, keepdims=False)
        current_f32 = current.astype(jnp.float32)
        square_sum = lax.psum(jnp.sum(current_f32 * current_f32, axis=1), ("row", "col"))
        first_in = (
            current_f32
            * lax.rsqrt(square_sum / D + norm_eps)[:, None]
            * gain_first.astype(jnp.float32)
        ).astype(jnp.bfloat16)
        shard_piece = lax.all_gather(first_in, "col", axis=1, tiled=True)
        query_part = product(shard_piece, query_proj)
        key_part = product(shard_piece, key_proj)
        value_part = product(shard_piece, value_proj)
        query_all, key_all, value_all = lax.psum((query_part, key_part, value_part), "row")
        first_row = lax.axis_index("row") * local_streams
        query_mine = lax.dynamic_slice_in_dim(query_all, first_row, local_streams, 0)
        key_mine = lax.dynamic_slice_in_dim(key_all, first_row, local_streams, 0)
        value_mine = lax.dynamic_slice_in_dim(value_all, first_row, local_streams, 0)
        attended = attention(
            query_mine.astype(jnp.bfloat16),
            key_mine.astype(jnp.bfloat16),
            value_mine.astype(jnp.bfloat16),
            cached_keys,
            cached_values,
            live_lengths,
        )
        head_terms = product(lax.all_gather(attended, "row", axis=0, tiled=True), output_proj)
        attn_mixed = lax.psum_scatter(head_terms, "col", scatter_dimension=1, tiled=True)
        after_attn = (current_f32 + attn_mixed).astype(jnp.bfloat16)
        after_f32 = after_attn.astype(jnp.float32)
        square_two = lax.psum(jnp.sum(after_f32 * after_f32, axis=1), ("row", "col"))
        second_in = (
            after_f32
            * lax.rsqrt(square_two / D + norm_eps)[:, None]
            * gain_second.astype(jnp.float32)
        ).astype(jnp.bfloat16)
        add_shard_piece = lax.all_gather(second_in, ("row", "col"), axis=1, tiled=True)
        gate_val = product(add_shard_piece, gate_proj)
        up_val = product(add_shard_piece, up_proj)
        activation = (jax.nn.silu(gate_val) * up_val).astype(jnp.bfloat16)
        ffn_mixed = lax.psum_scatter(
            product(activation, down_proj), ("row", "col"), scatter_dimension=1, tiled=True
        )
        current = (after_f32 + ffn_mixed).astype(jnp.bfloat16)
        current = shifted(current, "section", 1)
    return current[None]


def solution(mesh):
    return jax.shard_map(
        per_device,
        mesh=mesh,
        in_specs=(
            P("section", None, ("row", "col")),
            P(None, "row"),
            P("section", ("row", "col")),
            P("section", ("row", "col")),
            P("section", "row", "col"),
            P("section", "row", "col"),
            P("section", "row", "col"),
            P("section", "col", "row"),
            P("section", None, ("row", "col")),
            P("section", None, ("row", "col")),
            P("section", ("row", "col"), None),
            P("section", None, "row", "col", None, None),
            P("section", None, "row", "col", None, None),
        ),
        out_specs=P("section", None, ("row", "col")),
        check_vma=False,
    )
```

profile of v0, /device:TPU:1, one launch (start us, length us, event | category | flops | bytes accessed | tf_op | source)
XLA Modules:
  0.0 1437.7 jit_solution(12778658633375877881)
XLA Ops:
  8.2 63.8 %psum.140 = f32[64]{0:T(128)S(1)} all-reduce(f32[64]{0:T(128)S(1)} %fusion.168), channel_id=1, replica_groups=mesh['section'=4,'row'=8,'col'=4] {'row','col'}, use_global_device_ids=true, to_apply=%region_1.2 | all-reduce | flops 64 | bytes 512 | tf_op jit(solution)/shard_map/psum | solution.py:93
  72.9 9.1 all-gather
  85.7 33.8 %all-reduce.8 = (bf16[64,1280]{1,0:T(8,128)(2,1)}, bf16[64,256]{1,0:T(8,128)(2,1)}, bf16[64,256]{1,0:T(8,128)(2,1)}) all-reduce(f32[64,1280]{1,0:T(8,128)} %fusion.34, f32[64,256]{1,0:T(8,128)S(1)} %fusion.110, f32[64,256]{1,0:T(8,128)S(1)} %fusion.118), channel_id=1, replica_groups=mesh['section'=4,'row'=8,'col'=4] {'row'}, use_global_device_ids=true, to_apply=%region_2.3 | all-reduce | flops 114688 | bytes 688128 | tf_op jit(solution)/shard_map/psum | solution.py:103
  121.1 1.4 fusion.252
  124.7 16.1 %all_gather.37 = bf16[64,1280]{1,0:T(8,128)(2,1)S(1)} all-gather(bf16[8,1280]{1,0:T(8,128)(2,1)S(1)} %convert_element_type.245), channel_id=1, replica_groups=mesh['section'=4,'row'=8,'col'=4] {'row'}, dimensions={0}, use_global_device_ids=true | all-gather | bytes 184320 | tf_op jit(solution)/shard_map/all_gather | solution.py:116
  140.9 1.5 fusion.36
  142.4 17.3 %reduce-scatter.25.cloned.1.call-done = f32[160,64]{1,0:T(8,128)} async-done(((f32[640,64]{1,0:T(8,128)}), f32[160,64]{1,0:T(8,128)}) %reduce-scatter.25.cloned.1.call-update) | async-done | bytes 40976
  160.8 61.1 %psum.144 = f32[64]{0:T(128)S(1)} all-reduce(f32[64]{0:T(128)S(1)} %get-tuple-element.23), channel_id=1, replica_groups=mesh['section'=4,'row'=8,'col'=4] {'row','col'}, use_global_device_ids=true, to_apply=%region_9.10 | all-reduce | flops 64 | bytes 512 | tf_op jit(solution)/shard_map/psum | solution.py:120
  222.0 46.3 %all-gather.1 = bf16[32,160,64]{1,2,0:T(8,128)(2,1)S(1)} all-gather(bf16[1,160,64]{1,2,0:T(8,128)(2,1)S(1)} %fusion.199), channel_id=1, replica_groups=mesh['section'=4,'row'=8,'col'=4] {'row','col'}, dimensions={0}, use_global_device_ids=true | all-gather | bytes 675840 | tf_op jit(solution)/shard_map/all_gather | solution.py:126
  268.3 1.6 copy.41
  269.9 3.4 reshape.196
  273.2 3.7 fusion.18
  276.9 8.4 convolution_bitcast_fusion.3
  285.4 77.6 %reduce-scatter.27.cloned.1.call-done = f32[160,64]{1,0:T(8,128)} async-done(((f32[5120,64]{1,0:T(8,128)}), f32[160,64]{1,0:T(8,128)}) %reduce-scatter.27.cloned.1.call-update) | async-done | bytes 40976
  364.0 1.4 collective-permute-start
  365.4 2.7 collective-permute-done
  368.2 62.3 %psum.145 = f32[64]{0:T(128)S(1)} all-reduce(f32[64]{0:T(128)S(1)} %fusion.144), channel_id=1, replica_groups=mesh['section'=4,'row'=8,'col'=4] {'row','col'}, use_global_device_ids=true, to_apply=%region_12.13 | all-reduce | flops 64 | bytes 512 | tf_op jit(solution)/shard_map/psum | solution.py:93
  430.6 9.1 all-gather.2
  443.3 33.9 %all-reduce.9 = (bf16[64,1280]{1,0:T(8,128)(2,1)}, bf16[64,256]{1,0:T(8,128)(2,1)S(1)}, bf16[64,256]{1,0:T(8,128)(2,1)S(1)}) all-reduce(f32[64,1280]{1,0:T(8,128)} %fusion.32, f32[64,256]{1,0:T(8,128)S(1)} %fusion.108, f32[64,256]{1,0:T(8,128)S(1)} %fusion.116), channel_id=1, replica_groups=mesh['section'=4,'row'=8,'col'=4] {'row'}, use_global_device_ids=true, to_apply=%region_13.14 | all-reduce | flops 114688 | bytes 688128 | tf_op jit(solution)/shard_map/psum | solution.py:103
  478.1 1.4 fusion.253
  481.1 16.1 %all_gather.40 = bf16[64,1280]{1,0:T(8,128)(2,1)S(1)} all-gather(bf16[8,1280]{1,0:T(8,128)(2,1)S(1)} %convert_element_type.262), channel_id=1, replica_groups=mesh['section'=4,'row'=8,'col'=4] {'row'}, dimensions={0}, use_global_device_ids=true | all-gather | bytes 184320 | tf_op jit(solution)/shard_map/all_gather | solution.py:116
  497.3 1.5 fusion.39
  498.8 15.2 %reduce-scatter.29.cloned.1.call-done = f32[160,64]{1,0:T(8,128)} async-done(((f32[640,64]{1,0:T(8,128)}), f32[160,64]{1,0:T(8,128)}) %reduce-scatter.29.cloned.1.call-update) | async-done | bytes 40976
  515.1 61.1 %psum.149 = f32[64]{0:T(128)S(1)} all-reduce(f32[64]{0:T(128)S(1)} %get-tuple-element.21), channel_id=1, replica_groups=mesh['section'=4,'row'=8,'col'=4] {'row','col'}, use_global_device_ids=true, to_apply=%region_20.21 | all-reduce | flops 64 | bytes 512 | tf_op jit(solution)/shard_map/psum | solution.py:120
  576.3 46.3 %all-gather.3 = bf16[32,160,64]{1,2,0:T(8,128)(2,1)S(1)} all-gather(bf16[1,160,64]{1,2,0:T(8,128)(2,1)S(1)} %fusion.197), channel_id=1, replica_groups=mesh['section'=4,'row'=8,'col'=4] {'row','col'}, dimensions={0}, use_global_device_ids=true | all-gather | bytes 675840 | tf_op jit(solution)/shard_map/all_gather | solution.py:126
  622.6 1.6 copy.45
  624.1 3.4 reshape.200
  627.5 3.7 fusion.16
  631.2 8.4 convolution_bitcast_fusion.2
  639.7 77.6 %reduce-scatter.31.cloned.1.call-done = f32[160,64]{1,0:T(8,128)} async-done(((f32[5120,64]{1,0:T(8,128)}), f32[160,64]{1,0:T(8,128)}) %reduce-scatter.31.cloned.1.call-update) | async-done | bytes 40976
  718.3 1.4 collective-permute-start.1
  719.7 2.6 collective-permute-done.1
  722.4 62.3 %psum.150 = f32[64]{0:T(128)S(1)} all-reduce(f32[64]{0:T(128)S(1)} %fusion.152), channel_id=1, replica_groups=mesh['section'=4,'row'=8,'col'=4] {'row','col'}, use_global_device_ids=true, to_apply=%region_23.24 | all-reduce | flops 64 | bytes 512 | tf_op jit(solution)/shard_map/psum | solution.py:93
  784.8 9.1 all-gather.4
  797.5 33.8 %all-reduce.10 = (bf16[64,1280]{1,0:T(8,128)(2,1)}, bf16[64,256]{1,0:T(8,128)(2,1)S(1)}, bf16[64,256]{1,0:T(8,128)(2,1)S(1)}) all-reduce(f32[64,1280]{1,0:T(8,128)} %fusion.30, f32[64,256]{1,0:T(8,128)S(1)} %fusion.106, f32[64,256]{1,0:T(8,128)S(1)} %fusion.114), channel_id=1, replica_groups=mesh['section'=4,'row'=8,'col'=4] {'row'}, use_global_device_ids=true, to_apply=%region_24.25 | all-reduce | flops 114688 | bytes 688128 | tf_op jit(solution)/shard_map/psum | solution.py:103
  832.2 1.4 fusion.254
  835.2 16.3 %all_gather.43 = bf16[64,1280]{1,0:T(8,128)(2,1)S(1)} all-gather(bf16[8,1280]{1,0:T(8,128)(2,1)S(1)} %convert_element_type.279), channel_id=1, replica_groups=mesh['section'=4,'row'=8,'col'=4] {'row'}, dimensions={0}, use_global_device_ids=true | all-gather | bytes 184320 | tf_op jit(solution)/shard_map/all_gather | solution.py:116
  851.5 1.5 fusion.42
  853.1 15.2 %reduce-scatter.33.cloned.1.call-done = f32[160,64]{1,0:T(8,128)} async-done(((f32[640,64]{1,0:T(8,128)}), f32[160,64]{1,0:T(8,128)}) %reduce-scatter.33.cloned.1.call-update) | async-done | bytes 40976
  869.4 61.2 %psum.154 = f32[64]{0:T(128)S(1)} all-reduce(f32[64]{0:T(128)S(1)} %get-tuple-element.19), channel_id=1, replica_groups=mesh['section'=4,'row'=8,'col'=4] {'row','col'}, use_global_device_ids=true, to_apply=%region_31.32 | all-reduce | flops 64 | bytes 512 | tf_op jit(solution)/shard_map/psum | solution.py:120
  930.6 46.3 %all-gather.5 = bf16[32,160,64]{1,2,0:T(8,128)(2,1)S(1)} all-gather(bf16[1,160,64]{1,2,0:T(8,128)(2,1)S(1)} %fusion.195), channel_id=1, replica_groups=mesh['section'=4,'row'=8,'col'=4] {'row','col'}, dimensions={0}, use_global_device_ids=true | all-gather | bytes 675840 | tf_op jit(solution)/shard_map/all_gather | solution.py:126
  976.9 1.6 copy.49
  978.4 3.4 reshape.204
  981.8 3.7 fusion.14
  985.5 8.4 convolution_bitcast_fusion.1
  993.9 77.6 %reduce-scatter.35.cloned.1.call-done = f32[160,64]{1,0:T(8,128)} async-done(((f32[5120,64]{1,0:T(8,128)}), f32[160,64]{1,0:T(8,128)}) %reduce-scatter.35.cloned.1.call-update) | async-done | bytes 40976
  1072.6 1.3 collective-permute-start.2
  1073.9 2.7 collective-permute-done.2
  1076.7 62.3 %psum.155 = f32[64]{0:T(128)S(1)} all-reduce(f32[64]{0:T(128)S(1)} %fusion.160), channel_id=1, replica_groups=mesh['section'=4,'row'=8,'col'=4] {'row','col'}, use_global_device_ids=true, to_apply=%region_34.35 | all-reduce | flops 64 | bytes 512 | tf_op jit(solution)/shard_map/psum | solution.py:93
  1139.1 9.1 all-gather.6
  1151.8 33.8 %all-reduce.11 = (bf16[64,1280]{1,0:T(8,128)(2,1)}, bf16[64,256]{1,0:T(8,128)(2,1)S(1)}, bf16[64,256]{1,0:T(8,128)(2,1)S(1)}) all-reduce(f32[64,1280]{1,0:T(8,128)} %fusion.28, f32[64,256]{1,0:T(8,128)S(1)} %fusion.104, f32[64,256]{1,0:T(8,128)S(1)} %fusion.112), channel_id=1, replica_groups=mesh['section'=4,'row'=8,'col'=4] {'row'}, use_global_device_ids=true, to_apply=%region_35.36 | all-reduce | flops 114688 | bytes 688128 | tf_op jit(solution)/shard_map/psum | solution.py:103
  1186.5 1.4 fusion.255
  1189.5 16.1 %all_gather.46 = bf16[64,1280]{1,0:T(8,128)(2,1)S(1)} all-gather(bf16[8,1280]{1,0:T(8,128)(2,1)S(1)} %convert_element_type.296), channel_id=1, replica_groups=mesh['section'=4,'row'=8,'col'=4] {'row'}, dimensions={0}, use_global_device_ids=true | all-gather | bytes 184320 | tf_op jit(solution)/shard_map/all_gather | solution.py:116
  1205.6 1.5 fusion.45
  1207.1 15.2 %reduce-scatter.37.cloned.1.call-done = f32[160,64]{1,0:T(8,128)} async-done(((f32[640,64]{1,0:T(8,128)}), f32[160,64]{1,0:T(8,128)}) %reduce-scatter.37.cloned.1.call-update) | async-done | bytes 40976
  1223.4 61.1 %psum.159 = f32[64]{0:T(128)S(1)} all-reduce(f32[64]{0:T(128)S(1)} %get-tuple-element.17), channel_id=1, replica_groups=mesh['section'=4,'row'=8,'col'=4] {'row','col'}, use_global_device_ids=true, to_apply=%region_42.43 | all-reduce | flops 64 | bytes 512 | tf_op jit(solution)/shard_map/psum | solution.py:120
  1284.6 46.5 %all-gather.7 = bf16[32,160,64]{1,2,0:T(8,128)(2,1)S(1)} all-gather(bf16[1,160,64]{1,2,0:T(8,128)(2,1)S(1)} %fusion.193), channel_id=1, replica_groups=mesh['section'=4,'row'=8,'col'=4] {'row','col'}, dimensions={0}, use_global_device_ids=true | all-gather | bytes 675840 | tf_op jit(solution)/shard_map/all_gather | solution.py:126
  1331.2 1.6 copy.53
  1332.7 2.6 reshape.208
  1335.4 3.5 fusion.12
  1338.9 8.1 convolution_bitcast_fusion
  1347.1 77.7 %reduce-scatter.39.cloned.1.call-done = f32[160,64]{1,0:T(8,128)} async-done(((f32[5120,64]{1,0:T(8,128)}), f32[160,64]{1,0:T(8,128)}) %reduce-scatter.39.cloned.1.call-update) | async-done | bytes 40976
  1425.7 1.3 collective-permute-start.3
  1427.1 2.7 collective-permute-done.3
  (128 shorter events, 38.4 us)
Async XLA Ops:
  6.5 75.7 %copy-start = (bf16[1,640,1280]{2,1,0:T(8,128)(2,1)S(1)}, bf16[1,640,1280]{2,1,0:T(8,128)(2,1)}, u32[]{:S(2)}) copy-start(bf16[1,640,1280]{2,1,0:T(8,128)(2,1)} %param.17) | copy-start | bytes 4915204
  6.5 114.3 %copy-start.3 = (s32[4,8]{1,0:T(4,128)S(1)}, s32[4,8]{1,0:T(4,128)}, u32[]{:S(2)}) copy-start(s32[4,8]{1,0:T(4,128)} %param.14) | copy-start | bytes 388
  6.5 153.2 %reduce-scatter.25.cloned.1.call-start = ((), (), s32[]{:S(2)}) async-start(), calls=%async_computation.8 | async-start | bytes 409600
  82.3 58.6 %copy-start.1 = (bf16[1,1280,640]{2,1,0:T(8,128)(2,1)S(1)}, bf16[1,1280,640]{2,1,0:T(8,128)(2,1)}, u32[]{:S(2)}) copy-start(bf16[1,1280,640]{2,1,0:T(8,128)(2,1)} %param.20) | copy-start | bytes 4915204
  119.4 23.0 %copy-start.4 = (bf16[1,160]{1,0:T(2,128)(2,1)S(1)}, bf16[1,160]{1,0:T(2,128)(2,1)}, u32[]{:S(2)}) copy-start(bf16[1,160]{1,0:T(2,128)(2,1)} %param.16) | copy-start | bytes 964
  119.4 41.3 %copy-start.2 = (bf16[1,64,160]{2,1,0:T(8,128)(2,1)S(1)}, bf16[1,64,160]{2,1,0:T(8,128)(2,1)}, u32[]{:S(2)}) copy-start(bf16[1,64,160]{2,1,0:T(8,128)(2,1)} %param.13) | copy-start | bytes 61444
  142.4 220.6 %reduce-scatter.27.cloned.1.call-start = ((), (), s32[]{:S(2)}) async-start(), calls=%async_computation.9 | async-start | bytes 2703360
  285.3 228.7 %reduce-scatter.29.cloned.1.call-start = ((), (), s32[]{:S(2)}) async-start(), calls=%async_computation.10 | async-start | bytes 409600
  364.0 4.1 collective-permute-start
  498.7 218.5 %reduce-scatter.31.cloned.1.call-start = ((), (), s32[]{:S(2)}) async-start(), calls=%async_computation.11 | async-start | bytes 2703360
  639.6 228.7 %reduce-scatter.33.cloned.1.call-start = ((), (), s32[]{:S(2)}) async-start(), calls=%async_computation.12 | async-start | bytes 409600
  718.3 4.0 collective-permute-start.1
  853.0 218.5 %reduce-scatter.35.cloned.1.call-start = ((), (), s32[]{:S(2)}) async-start(), calls=%async_computation.13 | async-start | bytes 2703360
  993.9 228.4 %reduce-scatter.37.cloned.1.call-start = ((), (), s32[]{:S(2)}) async-start(), calls=%async_computation.14 | async-start | bytes 409600
  1072.6 4.0 collective-permute-start.2
  1207.1 217.7 %reduce-scatter.39.cloned.1.call-start = ((), (), s32[]{:S(2)}) async-start(), calls=%async_computation.15 | async-start | bytes 2703360
  1425.7 4.0 collective-permute-start.3
Sparse Core Ops, SparseCore 0:
  142.5 17.1 reduce-scatter.24
  285.4 77.5 reduce-scatter.26
  498.9 15.0 reduce-scatter.28
  639.7 77.4 reduce-scatter.30
  853.1 15.0 reduce-scatter.32
  994.0 77.5 reduce-scatter.34
  1207.2 15.0 reduce-scatter.36
  1347.2 77.5 reduce-scatter.38
where the time goes:
time: 1450 us; the launch traced here: 1440 us
  blocking collectives  917 us (63%)
  waiting for transfers between devices  384 us (26%)
  matrix products  78.4 us (5%)
  local copies, waits for them, and re-layouts  32.1 us (2%)
  between operations  14.5 us (1%)
    unnamed x16, waiting for transfers between devices  374 us
    psum x4, blocking collectives, per_device(): lax.psum(jnp.sum(current_f32 * current_f32, axis=1), ('row', 'col'))  251 us
    psum x4, blocking collectives, per_device(): lax.psum(jnp.sum(after_f32 * after_f32, axis=1), ('row', 'col'))  245 us
    all_gather x4, blocking collectives, per_device(): lax.all_gather(second_in, ('row', 'col'), axis=1, tiled=True)  185 us
    psum x4, blocking collectives, per_device(): lax.psum((query_part, key_part, value_part), 'row')  135 us
    all_gather x4, blocking collectives, per_device(): lax.all_gather(attended, 'row', axis=0, tiled=True)  64.7 us
    unnamed x8, matrix products  39 us
    all_gather x4, blocking collectives, per_device(): shard_piece = lax.all_gather(first_in, 'col', axis=1, tiled=True)  36.4 us
  transfers between devices with their start and end apart: 12, of which 12 were waited for; matrix products, arithmetic and copies ran while one was open for 0% of the time, Pallas kernels for 0%

commit v1 on v0

v1 whole, which is shorter than its diff:
```python
import functools
import math

import jax
import jax.numpy as jnp
from jax import lax
from jax.experimental import pallas as pl
from jax.experimental.pallas import tpu as pltpu
from jax.sharding import PartitionSpec as P

D = 5120
HD = 128
CTX = 96
TURNS = 4
ROWS = 8
COLS = 4
GROUP = ROWS * COLS
WIDE = 640
PIECE = 160
SUB = 16
STREAMS = 64
LOCAL = 8
QKV = 1792
HALF = 896
HIDDEN = 512
norm_eps = 1e-06
masked_score = -1e30
f32 = jnp.float32
bf16 = jnp.bfloat16


def remote(src, dst, send, recv, device):
    return pltpu.make_async_remote_copy(
        src_ref=src,
        dst_ref=dst,
        send_sem=send,
        recv_sem=recv,
        device_id=device,
        device_id_type=pl.DeviceIdType.MESH,
    )


def kernel(
    len_ref,
    hid_ref,
    ag_ref,
    fg_ref,
    wq_hbm,
    wk_hbm,
    wv_hbm,
    wo_hbm,
    wg_hbm,
    wu_hbm,
    wd_hbm,
    kc_hbm,
    vc_hbm,
    out_ref,
    wqkv,
    wo,
    wgu,
    wd,
    kc,
    vc,
    init,
    gain1,
    gain2,
    bias,
    xin,
    s2,
    r2,
    o3,
    s4,
    r4,
    x2_all,
    acc,
    s6,
    r6,
    x_send,
    wsem,
    csem,
    send0,
    recv0,
    sendg,
    recvg,
    send1,
    recv1,
    send2,
    recv2,
    send3,
    recv3,
    send4,
    recv4,
    send5,
    recv5,
    send6,
    recv6,
):
    s = lax.axis_index("section")
    r = lax.axis_index("row")
    c = lax.axis_index("col")
    me = r * COLS + c
    x_chip = r // 2
    s_next = lax.rem(s + 1, TURNS)
    s_prev = lax.rem(s + TURNS - 1, TURNS)

    def row_at(i):
        return lax.rem(r + i, ROWS)

    def col_at(i):
        return lax.rem(c + i, COLS)

    weight_copies = [
        pltpu.make_async_copy(wq_hbm.at[0], wqkv.at[:, pl.ds(0, 1280)], wsem.at[0]),
        pltpu.make_async_copy(wk_hbm.at[0], wqkv.at[:, pl.ds(1280, 256)], wsem.at[1]),
        pltpu.make_async_copy(wv_hbm.at[0], wqkv.at[:, pl.ds(1536, 256)], wsem.at[2]),
        pltpu.make_async_copy(wo_hbm.at[0], wo, wsem.at[3]),
        pltpu.make_async_copy(wg_hbm.at[0], wgu.at[:, pl.ds(0, HIDDEN)], wsem.at[4]),
        pltpu.make_async_copy(wu_hbm.at[0], wgu.at[:, pl.ds(HIDDEN, HIDDEN)], wsem.at[5]),
        pltpu.make_async_copy(wd_hbm.at[0], wd, wsem.at[6]),
    ]

    def cache_copies(t):
        m = lax.rem(s + TURNS - t, TURNS)
        copies = []
        for g in range(2):
            copies.append(
                pltpu.make_async_copy(kc_hbm.at[0, m, :, g], kc.at[t, g], csem.at[t, g])
            )
            copies.append(
                pltpu.make_async_copy(vc_hbm.at[0, m, :, g], vc.at[t, g], csem.at[t, 2 + g])
            )
        return copies

    for copy in weight_copies[:3]:
        copy.start()
    for copy in cache_copies(0):
        copy.start()
    for copy in weight_copies[3:]:
        copy.start()
    for t in range(1, TURNS):
        for copy in cache_copies(t):
            copy.start()

    barrier = pltpu.get_barrier_semaphore()

    def greet(i, _):
        other = lax.rem(me + i, GROUP)
        pl.semaphore_signal(
            barrier,
            inc=1,
            device_id=(s, other // COLS, lax.rem(other, COLS)),
            device_id_type=pl.DeviceIdType.MESH,
        )
        return 0

    lax.fori_loop(1, GROUP, greet, 0)
    for i in range(COLS):
        pl.semaphore_signal(
            barrier, inc=1, device_id=(s_prev, r, i), device_id_type=pl.DeviceIdType.MESH
        )

    init[c] = jnp.zeros((80, 256), bf16)
    init[c, 0:64, 0:PIECE] = hid_ref[0]
    gain_row = lax.broadcasted_iota(jnp.int32, (SUB, PIECE), 0)
    init[c, 64:80, 0:PIECE] = jnp.where(
        gain_row == 0, ag_ref[...].astype(f32), fg_ref[...].astype(f32)
    ).astype(bf16)

    stream_row = lax.broadcasted_iota(jnp.int32, (LOCAL, LOCAL * CTX), 0)
    position = lax.broadcasted_iota(jnp.int32, (LOCAL, LOCAL * CTX), 1)
    for t in range(TURNS):
        m = lax.rem(s + TURNS - t, TURNS)
        offsets = jnp.full((LOCAL, LOCAL * CTX), masked_score, f32)
        for b in range(LOCAL):
            live = (
                (stream_row == b)
                & (position >= b * CTX)
                & (position < b * CTX + len_ref[m, b])
            )
            offsets = jnp.where(live, 0.0, offsets)
        bias[t] = offsets

    pl.semaphore_wait(barrier, GROUP - 1 + COLS)

    def send_init(i):
        return remote(
            init.at[c], init.at[c], send0.at[i], recv0.at[c], (s, r, col_at(i))
        )

    def wait_init(i):
        return remote(
            init.at[col_at(i)], init.at[col_at(i)], send0.at[i], recv0.at[col_at(i)],
            (s, r, col_at(i)),
        )

    for i in range(1, COLS):
        send_init(i).start()
    for i in range(1, COLS):
        wait_init(i).wait_recv()
    joined = None
    for i in range(COLS):
        piece = jnp.concatenate(
            [init[i].astype(f32), jnp.zeros((80, WIDE - 256), f32)], axis=1
        )
        if i:
            piece = pltpu.roll(piece, i * PIECE, 1)
        joined = piece if joined is None else joined + piece
    xin[0] = joined[0:64].astype(bf16).reshape(COLS, SUB, WIDE)
    gain1[...] = joined[64:65]
    gain2[r] = jnp.broadcast_to(joined[65:66], (8, WIDE))

    def send_gain(i):
        return remote(
            gain2.at[r], gain2.at[r], sendg.at[i], recvg.at[r], (s, row_at(i), c)
        )

    def wait_gain(i):
        return remote(
            gain2.at[row_at(i)], gain2.at[row_at(i)], sendg.at[i], recvg.at[row_at(i)],
            (s, row_at(i), c),
        )

    def turn(t, _):
        x_all = xin[t].reshape(STREAMS, WIDE).astype(f32)
        squares = jnp.sum(x_all * x_all, axis=1, keepdims=True)
        high = squares.astype(bf16).astype(f32)
        low = squares - high
        left = (x_all * gain1[...]).astype(bf16)

        @pl.when(t == 0)
        def _():
            for copy in weight_copies[:3]:
                copy.wait()

        part = jnp.dot(left, wqkv[...], preferred_element_type=f32)
        part = part.reshape(ROWS, LOCAL, QKV)
        s2[:, :, 0:HALF] = jnp.concatenate(
            [part[:, :, 0:HALF], part[:, :, HALF:QKV]], axis=1
        ).astype(bf16)
        s2[:, :, HALF:1024] = jnp.broadcast_to(
            jnp.concatenate(
                [high.reshape(ROWS, LOCAL, 1), low.reshape(ROWS, LOCAL, 1)], axis=1
            ),
            (ROWS, SUB, 128),
        ).astype(bf16)

        def send_two(i):
            return remote(
                s2.at[row_at(i)], r2.at[r], send2.at[i], recv2.at[r], (s, row_at(i), c)
            )

        def wait_two(i):
            return remote(
                s2.at[row_at(i)], r2.at[row_at(i)], send2.at[i], recv2.at[row_at(i)],
                (s, row_at(i), c),
            )

        for i in (4, 3, 5, 2, 6, 1, 7):
            send_two(i).start()

        @pl.when(t == 0)
        def _():
            for i in range(1, ROWS):
                send_gain(i).start()

        total = s2[r].astype(f32)
        for i in (1, 7, 2, 6, 3, 5, 4):
            wait_two(i).wait_recv()
            total = total + r2[row_at(i)].astype(f32)
        mean_square = (total[0:8, HALF:HALF + 1] + total[8:16, HALF:HALF + 1]) / D
        scale = lax.rsqrt(mean_square + norm_eps)
        top = (total[0:8, 0:HALF] * scale).astype(bf16).astype(f32)
        bottom = (total[8:16, 0:HALF] * scale).astype(bf16).astype(f32)

        def head(j):
            if j < 7:
                return top[:, j * HD:(j + 1) * HD]
            return bottom[:, (j - 7) * HD:(j - 6) * HD]

        @pl.when(t == 0)
        def _():
            for copy in cache_copies(0):
                copy.wait()

        @pl.when(t > 0)
        def _():
            for copy in cache_copies(t):
                copy.wait()

        score_scale = 1.0 / math.sqrt(HD)
        offsets = jnp.concatenate([bias[t]] * 5, axis=0)
        mixed_rows = []
        for g in range(2):
            queries = jnp.concatenate([head(5 * g + j) for j in range(5)], axis=0)
            key_new = jnp.concatenate([head(10 + g)] * 5, axis=0)
            value_new = jnp.concatenate([head(12 + g)] * 5, axis=0)
            keys = kc[t, g].reshape(LOCAL * CTX, HD)
            values = vc[t, g].reshape(LOCAL * CTX, HD)
            scores = lax.dot_general(
                queries.astype(bf16), keys, (((1,), (1,)), ((), ())),
                preferred_element_type=f32,
            )
            scores = scores * score_scale + offsets
            self_score = jnp.sum(queries * key_new, axis=1, keepdims=True) * score_scale
            row_max = jnp.maximum(jnp.max(scores, axis=1, keepdims=True), self_score)
            weights = jnp.exp(scores - row_max)
            self_weight = jnp.exp(self_score - row_max)
            denominator = jnp.sum(weights, axis=1, keepdims=True) + self_weight
            probs = (weights / denominator).astype(bf16)
            self_prob = (self_weight / denominator).astype(bf16).astype(f32)
            mixed = jnp.dot(probs, values, preferred_element_type=f32)
            mixed = mixed + self_prob * value_new
            mixed_rows.append(
                jnp.concatenate([mixed[j * 8:(j + 1) * 8] for j in range(5)], axis=1)
            )
        o3[r] = jnp.concatenate(mixed_rows, axis=0).astype(bf16)

        def send_three(i):
            return remote(
                o3.at[r], o3.at[r], send3.at[i], recv3.at[r], (s, row_at(i), c)
            )

        def wait_three(i):
            return remote(
                o3.at[row_at(i)], o3.at[row_at(i)], send3.at[i], recv3.at[row_at(i)],
                (s, row_at(i), c),
            )

        for i in (4, 3, 5, 2, 6, 1, 7):
            send_three(i).start()

        @pl.when(t == 0)
        def _():
            weight_copies[3].wait()

        for i in (1, 7, 2, 6, 3, 5, 4):
            wait_three(i).wait_recv()
        gathered = o3[...].astype(f32)
        heads = jnp.concatenate(
            [gathered[:, 0:8].reshape(STREAMS, WIDE), gathered[:, 8:16].reshape(STREAMS, WIDE)],
            axis=1,
        ).astype(bf16)
        out_part = jnp.dot(heads, wo[...], preferred_element_type=f32)
        s4[...] = out_part.astype(bf16).reshape(COLS, SUB, WIDE)

        def send_four(i):
            return remote(
                s4.at[col_at(i)], r4.at[c], send4.at[i], recv4.at[c], (s, r, col_at(i))
            )

        def wait_four(i):
            return remote(
                s4.at[col_at(i)], r4.at[col_at(i)], send4.at[i], recv4.at[col_at(i)],
                (s, r, col_at(i)),
            )

        for i in (2, 1, 3):
            send_four(i).start()
        after = xin[t, c].astype(f32) + s4[c].astype(f32)
        for i in (1, 3, 2):
            wait_four(i).wait_recv()
            after = after + r4[col_at(i)].astype(f32)
        x2_all[r, c] = after.astype(bf16)
        after = x2_all[r, c].astype(f32)

        def send_five(i, _):
            other = lax.rem(me + i, GROUP)
            remote(
                x2_all.at[r, c], x2_all.at[r, c], send5.at[i], recv5.at[me],
                (s, other // COLS, lax.rem(other, COLS)),
            ).start()
            return 0

        lax.fori_loop(1, GROUP, send_five, 0)

        @pl.when(t == 0)
        def _():
            for i in range(1, ROWS):
                wait_gain(i).wait_recv()
            for copy in weight_copies[4:6]:
                copy.wait()

        acc[...] = jnp.zeros_like(acc)

        def chip_at(j):
            return lax.rem(x_chip + j + (j // 2) * (5 - 2 * j), 4)

        def gate_step(j, squares):
            xc = chip_at(j)
            for k in range(2):
                for q in range(COLS):
                    row = 2 * xc + k
                    src = row * COLS + q

                    @pl.when(src != me)
                    def _():
                        remote(
                            x2_all.at[row, q], x2_all.at[row, q], send5.at[0],
                            recv5.at[src], (s, row, q),
                        ).wait_recv()

            values = jnp.concatenate(
                [x2_all[2 * xc + k].reshape(STREAMS, WIDE) for k in range(2)], axis=1
            ).astype(f32)
            gains = jnp.concatenate([gain2[2 * xc + k, 0:1] for k in range(2)], axis=1)
            square = values * values
            for k in range(10):
                squares = squares + square[:, k * 128:(k + 1) * 128]
            scaled = (values * gains).astype(bf16)
            first = pl.multiple_of(xc * 1280, 1280)
            acc[...] += jnp.dot(
                scaled, wgu[pl.ds(first, 1280), :], preferred_element_type=f32
            )
            return squares

        squares = lax.fori_loop(0, 4, gate_step, jnp.zeros((STREAMS, 128), f32))
        mean_square = jnp.sum(squares, axis=1, keepdims=True) / D
        scale = lax.rsqrt(mean_square + norm_eps)
        gate = acc[:, 0:HIDDEN] * scale
        up = acc[:, HIDDEN:2 * HIDDEN] * scale
        activation = (gate / (1.0 + jnp.exp(-gate)) * up).astype(bf16)

        @pl.when(t == 0)
        def _():
            weight_copies[6].wait()

        def down_step(j, _):
            xc = chip_at(3 - j)
            first = pl.multiple_of(xc * 1280, 1280)
            part = jnp.dot(
                activation, wd[:, pl.ds(first, 1280)], preferred_element_type=f32
            ).astype(bf16)
            for k in range(2):
                s6[2 * xc + k] = part[:, k * WIDE:(k + 1) * WIDE].reshape(COLS, SUB, WIDE)
            for k in range(2):
                for q in range(COLS):
                    row = 2 * xc + k
                    dst = row * COLS + q

                    @pl.when(dst != me)
                    def _():
                        remote(
                            s6.at[row, q], r6.at[r, c], send6.at[dst], recv6.at[me],
                            (s, row, q),
                        ).start()

            return 0

        lax.fori_loop(0, 4, down_step, 0)

        def sum_six(i, total):
            other = lax.rem(me + i, GROUP)
            row, q = other // COLS, lax.rem(other, COLS)
            remote(
                s6.at[row, q], r6.at[row, q], send6.at[other], recv6.at[other], (s, row, q)
            ).wait_recv()
            return total + r6[row, q].astype(f32)

        total = lax.fori_loop(1, GROUP, sum_six, after + s6[r, c].astype(f32))
        x_send[...] = total.astype(bf16)

        def send_one(i):
            return remote(
                x_send, xin.at[t + 1, c], send1.at[i], recv1.at[t, c],
                (s_next, r, col_at(i)),
            )

        def wait_one(i):
            return remote(
                x_send, xin.at[t + 1, col_at(i)], send1.at[i], recv1.at[t, col_at(i)],
                (s_next, r, col_at(i)),
            )

        for i in range(COLS):
            send_one(i).start()

        for i in range(1, ROWS):
            send_two(i).wait_send()
            send_three(i).wait_send()
        for i in range(1, COLS):
            send_four(i).wait_send()

        def finish(i, _):
            other = lax.rem(me + i, GROUP)
            row, q = other // COLS, lax.rem(other, COLS)
            remote(
                x2_all.at[r, c], x2_all.at[r, c], send5.at[i], recv5.at[me], (s, row, q)
            ).wait_send()
            remote(
                s6.at[row, q], r6.at[r, c], send6.at[other], recv6.at[me], (s, row, q)
            ).wait_send()
            return 0

        lax.fori_loop(1, GROUP, finish, 0)
        for i in range(COLS):
            send_one(i).wait_send()
        for i in range(COLS):
            wait_one(i).wait_recv()
        return 0

    lax.fori_loop(0, TURNS, turn, 0)

    final = xin[TURNS].reshape(STREAMS, WIDE).astype(f32)
    final = pltpu.roll(final, lax.rem(WIDE - c * PIECE, WIDE), 1)
    out_ref[0] = final[:, 0:PIECE].astype(bf16)
    for i in range(1, COLS):
        send_init(i).wait_send()
    for i in range(1, ROWS):
        send_gain(i).wait_send()


def per_device(
    hidden,
    lengths,
    attn_gain,
    ffn_gain,
    q_weight,
    key_weight,
    value_weight,
    out_weight,
    gate_weight,
    up_weight,
    down_weight,
    key_cache,
    value_cache,
):
    vmem = pl.BlockSpec(memory_space=pltpu.VMEM)
    hbm = pl.BlockSpec(memory_space=pl.ANY)
    dma = pltpu.SemaphoreType.DMA
    return pl.pallas_call(
        kernel,
        out_shape=jax.ShapeDtypeStruct((1, STREAMS, PIECE), bf16),
        in_specs=[pl.BlockSpec(memory_space=pltpu.SMEM), vmem, vmem, vmem] + [hbm] * 9,
        out_specs=vmem,
        scratch_shapes=[
            pltpu.VMEM((WIDE, QKV), bf16),
            pltpu.VMEM((1280, WIDE), bf16),
            pltpu.VMEM((D, 2 * HIDDEN), bf16),
            pltpu.VMEM((HIDDEN, D), bf16),
            pltpu.VMEM((TURNS, 2, LOCAL, CTX, HD), bf16),
            pltpu.VMEM((TURNS, 2, LOCAL, CTX, HD), bf16),
            pltpu.VMEM((COLS, 80, 256), bf16),
            pltpu.VMEM((1, WIDE), f32),
            pltpu.VMEM((ROWS, 8, WIDE), f32),
            pltpu.VMEM((TURNS, LOCAL, LOCAL * CTX), f32),
            pltpu.VMEM((TURNS + 1, COLS, SUB, WIDE), bf16),
            pltpu.VMEM((ROWS, SUB, 1024), bf16),
            pltpu.VMEM((ROWS, SUB, 1024), bf16),
            pltpu.VMEM((ROWS, SUB, WIDE), bf16),
            pltpu.VMEM((COLS, SUB, WIDE), bf16),
            pltpu.VMEM((COLS, SUB, WIDE), bf16),
            pltpu.VMEM((ROWS, COLS, SUB, WIDE), bf16),
            pltpu.VMEM((STREAMS, 2 * HIDDEN), f32),
            pltpu.VMEM((ROWS, COLS, SUB, WIDE), bf16),
            pltpu.VMEM((ROWS, COLS, SUB, WIDE), bf16),
            pltpu.VMEM((SUB, WIDE), bf16),
            dma((7,)),
            dma((TURNS, 4)),
            dma((COLS,)),
            dma((COLS,)),
            dma((ROWS,)),
            dma((ROWS,)),
            dma((COLS,)),
            dma((TURNS, COLS)),
            dma((ROWS,)),
            dma((ROWS,)),
            dma((ROWS,)),
            dma((ROWS,)),
            dma((COLS,)),
            dma((COLS,)),
            dma((GROUP,)),
            dma((GROUP,)),
            dma((GROUP,)),
            dma((GROUP,)),
        ],
        compiler_params=pltpu.CompilerParams(
            collective_id=0, has_side_effects=True, vmem_limit_bytes=56 * 1024 * 1024
        ),
        cost_estimate=pl.CostEstimate(
            flops=TURNS * 2 * STREAMS * 9830400, bytes_accessed=24_000_000, transcendentals=0
        ),
    )(
        lengths,
        hidden,
        attn_gain,
        ffn_gain,
        q_weight,
        key_weight,
        value_weight,
        out_weight,
        gate_weight,
        up_weight,
        down_weight,
        key_cache,
        value_cache,
    )


def solution(mesh):
    return jax.shard_map(
        per_device,
        mesh=mesh,
        in_specs=(
            P("section", None, ("row", "col")),
            P(None, "row"),
            P("section", ("row", "col")),
            P("section", ("row", "col")),
            P("section", "row", "col"),
            P("section", "row", "col"),
            P("section", "row", "col"),
            P("section", "col", "row"),
            P("section", None, ("row", "col")),
            P("section", None, ("row", "col")),
            P("section", ("row", "col"), None),
            P("section", None, "row", "col", None, None),
            P("section", None, "row", "col", None, None),
        ),
        out_specs=P("section", None, ("row", "col")),
        check_vma=False,
    )
```

time: 1450 us -> 181 us (0.12)
  blocking collectives: 917 us -> 0 us
  waiting for transfers between devices: 384 us -> 0 us
  Pallas kernels: 0 us -> 179 us
  matrix products: 78.4 us -> 0 us
  local copies, waits for them, and re-layouts: 32.1 us -> 1.38 us
    psum x12 -> x0, blocking collectives: 631 us -> none  [the longest x4 251 us: per_device(): lax.psum(jnp.sum(current_f32 * current_f32, axis=1), ('row', 'col'))]
    unnamed x16 -> x0, waiting for transfers between devices: 374 us -> none
    all_gather x12 -> x0, blocking collectives: 286 us -> none  [the longest x4 185 us: per_device(): lax.all_gather(second_in, ('row', 'col'), axis=1, tiled=True)]
    pallas_call x0 -> x1, Pallas kernels: none -> 179 us  [per_device(): pl.pallas_call(kernel, out_shape=jax.ShapeDtypeStruct((1, STREAMS, PIECE)...]
    dot_general x28 -> x0, matrix products: 39.3 us -> none  [the longest x16 28.1 us: product(): return jnp.dot(left, right, preferred_element_type=jnp.float32)]
    unnamed x8 -> x0, matrix products: 39 us -> none
    unnamed x27 -> x1, local copies, waits for them, and re-layouts: 21.6 us -> 1.38 us
  transfers between devices with their start and end apart: 12 -> 0, of which waited for: 12 -> 0; matrix products, arithmetic and copies ran while one was open for 0% -> 0% of each run, Pallas kernels for 0% -> 0%
where the time goes in v1:
time: 181 us
  Pallas kernels  179 us (99%)
    pallas_call x1, Pallas kernels, per_device(): pl.pallas_call(kernel, out_shape=jax.ShapeDtypeStruct((1, STREAMS, PIECE)...  179 us

profile of v1, /device:TPU:1, one launch (start us, length us, event | category | flops | bytes accessed | tf_op | source)
XLA Modules:
  0.0 180.7 jit_solution(1074445560079070326)
XLA Ops:
  0.0 179.3 %shard_map.127 = bf16[1,64,160]{2,1,0:T(8,128)(2,1)} custom-call(s32[4,8]{1,0:T(4,128)} %len_ref.1, bf16[1,64,160]{2,1,0:T(8,128)(2,1)} %hid_ref.1, bf16[1,160]{1,0:T(2,128)(2,1)} %ag_ref.1, bf16[1,160]{1,0:T(2,128)(2,1)} %fg_ref.1, bf16[1,640,1280]{2,1,0:T(8,128)(2,1)} %wq_hbm.1, bf16[1,640,256]{2,1,0:T(8,128)(2,1)} %wk_hbm.1, bf16[1,640,256]{2,1,0:T(8,128)(2,1)} %wv_hbm.1, ...), custom_call_target="tpu_custom_call" | custom-call | flops 5033164800 | bytes 24000000 | tf_op jit(solution)/shard_map/pallas_call | solution.py:530
  179.3 1.4 copy.15

commit v2 on v1

--- a/solution.py
+++ b/solution.py
@@ -14,7 +14,8 @@
 TURNS = 4
 ROWS = 8
 COLS = 4
-GROUP = ROWS * COLS
+CHIPS = 4
+PEERS = 16
 WIDE = 640
 PIECE = 160
 SUB = 16
@@ -73,6 +74,9 @@
     r4,
     x2_all,
     acc,
+    keep,
+    p6,
+    q6,
     s6,
     r6,
     x_send,
@@ -92,14 +96,19 @@
     recv4,
     send5,
     recv5,
+    send_f,
+    recv_f,
+    send_p,
+    recv_p,
     send6,
     recv6,
 ):
     s = lax.axis_index("section")
     r = lax.axis_index("row")
     c = lax.axis_index("col")
-    me = r * COLS + c
     x_chip = r // 2
+    core = lax.rem(r, 2)
+    pair = 2 * x_chip + 1 - core
     s_next = lax.rem(s + 1, TURNS)
     s_prev = lax.rem(s + TURNS - 1, TURNS)
 
@@ -143,20 +152,15 @@
 
     barrier = pltpu.get_barrier_semaphore()
 
-    def greet(i, _):
-        other = lax.rem(me + i, GROUP)
+    def row_of(dx):
+        return 2 * lax.rem(x_chip + dx, CHIPS) + core
+
+    greeted = [(s, row_of(i // COLS), col_at(i % COLS)) for i in range(1, PEERS)]
+    greeted += [(s, 2 * lax.rem(x_chip + i, CHIPS) + 1 - core, c) for i in range(CHIPS)]
+    greeted += [(s_prev, r, i) for i in range(COLS)]
+    for device in greeted:
         pl.semaphore_signal(
-            barrier,
-            inc=1,
-            device_id=(s, other // COLS, lax.rem(other, COLS)),
-            device_id_type=pl.DeviceIdType.MESH,
-        )
-        return 0
-
-    lax.fori_loop(1, GROUP, greet, 0)
-    for i in range(COLS):
-        pl.semaphore_signal(
-            barrier, inc=1, device_id=(s_prev, r, i), device_id_type=pl.DeviceIdType.MESH
+            barrier, inc=1, device_id=device, device_id_type=pl.DeviceIdType.MESH
         )
 
     init[c] = jnp.zeros((80, 256), bf16)
@@ -180,7 +184,7 @@
             offsets = jnp.where(live, 0.0, offsets)
         bias[t] = offsets
 
-    pl.semaphore_wait(barrier, GROUP - 1 + COLS)
+    pl.semaphore_wait(barrier, len(greeted))
 
     def send_init(i):
         return remote(
@@ -363,15 +367,14 @@
         x2_all[r, c] = after.astype(bf16)
         after = x2_all[r, c].astype(f32)
 
-        def send_five(i, _):
-            other = lax.rem(me + i, GROUP)
-            remote(
-                x2_all.at[r, c], x2_all.at[r, c], send5.at[i], recv5.at[me],
-                (s, other // COLS, lax.rem(other, COLS)),
-            ).start()
-            return 0
-
-        lax.fori_loop(1, GROUP, send_five, 0)
+        def send_five(i):
+            return remote(
+                x2_all.at[r, c], x2_all.at[r, c], send5.at[i], recv5.at[x_chip, c],
+                (s, row_of(i // COLS), col_at(i % COLS)),
+            )
+
+        for i in (2, 1, 3, 6, 14, 5, 7, 13, 15, 4, 12, 10, 9, 11, 8):
+            send_five(i).start()
 
         @pl.when(t == 0)
         def _():
@@ -385,20 +388,36 @@
         def chip_at(j):
             return lax.rem(x_chip + j + (j // 2) * (5 - 2 * j), 4)
 
+        def forward(xc):
+            row = 2 * xc + core
+            return remote(
+                x2_all.at[row], x2_all.at[row], send_f.at[xc], recv_f.at[xc], (s, pair, c)
+            )
+
+        def collect(j):
+            xc = chip_at(j)
+            for q in range(COLS):
+
+                @pl.when((xc != x_chip) | (q != c))
+                def _():
+                    row = 2 * xc + core
+                    remote(
+                        x2_all.at[row, q], x2_all.at[row, q], send5.at[0],
+                        recv5.at[xc, q], (s, pair, c),
+                    ).wait_recv()
+
+            forward(xc).start()
+
         def gate_step(j, squares):
+            @pl.when(j < CHIPS - 1)
+            def _():
+                collect(j + 1)
+
             xc = chip_at(j)
-            for k in range(2):
-                for q in range(COLS):
-                    row = 2 * xc + k
-                    src = row * COLS + q
-
-                    @pl.when(src != me)
-                    def _():
-                        remote(
-                            x2_all.at[row, q], x2_all.at[row, q], send5.at[0],
-                            recv5.at[src], (s, row, q),
-                        ).wait_recv()
-
+            row = 2 * xc + 1 - core
+            remote(
+                x2_all.at[row], x2_all.at[row], send_f.at[xc], recv_f.at[xc], (s, pair, c)
+            ).wait_recv()
             values = jnp.concatenate(
                 [x2_all[2 * xc + k].reshape(STREAMS, WIDE) for k in range(2)], axis=1
             ).astype(f32)
@@ -413,7 +432,8 @@
             )
             return squares
 
-        squares = lax.fori_loop(0, 4, gate_step, jnp.zeros((STREAMS, 128), f32))
+        collect(0)
+        squares = lax.fori_loop(0, CHIPS, gate_step, jnp.zeros((STREAMS, 128), f32))
         mean_square = jnp.sum(squares, axis=1, keepdims=True) / D
         scale = lax.rsqrt(mean_square + norm_eps)
         gate = acc[:, 0:HIDDEN] * scale
@@ -424,39 +444,69 @@
         def _():
             weight_copies[6].wait()
 
+        def swap(xc):
+            return remote(
+                p6.at[xc], q6.at[xc], send_p.at[xc], recv_p.at[xc], (s, pair, c)
+            )
+
         def down_step(j, _):
-            xc = chip_at(3 - j)
+            xc = chip_at(CHIPS - 1 - j)
             first = pl.multiple_of(xc * 1280, 1280)
             part = jnp.dot(
                 activation, wd[:, pl.ds(first, 1280)], preferred_element_type=f32
-            ).astype(bf16)
-            for k in range(2):
-                s6[2 * xc + k] = part[:, k * WIDE:(k + 1) * WIDE].reshape(COLS, SUB, WIDE)
-            for k in range(2):
-                for q in range(COLS):
-                    row = 2 * xc + k
-                    dst = row * COLS + q
-
-                    @pl.when(dst != me)
-                    def _():
-                        remote(
-                            s6.at[row, q], r6.at[r, c], send6.at[dst], recv6.at[me],
-                            (s, row, q),
-                        ).start()
-
+            )
+            lower, upper = part[:, 0:WIDE], part[:, WIDE:1280]
+            keep[xc] = jnp.where(core == 0, lower, upper)
+            p6[xc] = jnp.where(core == 0, upper, lower).astype(bf16)
+            swap(xc).start()
             return 0
 
-        lax.fori_loop(0, 4, down_step, 0)
-
-        def sum_six(i, total):
-            other = lax.rem(me + i, GROUP)
-            row, q = other // COLS, lax.rem(other, COLS)
+        lax.fori_loop(0, CHIPS, down_step, 0)
+
+        def send_six(xc, i):
+            q = col_at(i)
+            return remote(
+                s6.at[xc, q], r6.at[x_chip, c], send6.at[xc, i], recv6.at[x_chip, c],
+                (s, 2 * xc + core, q),
+            )
+
+        def share_step(j, _):
+            xc = chip_at(CHIPS - 1 - j)
+            swap(xc).wait_recv()
+            both = keep[xc] + q6[xc].astype(f32)
+            s6[xc] = both.astype(bf16).reshape(COLS, SUB, WIDE)
+            for i in (2, 1, 3):
+                send_six(xc, i).start()
+
+            @pl.when(xc != x_chip)
+            def _():
+                send_six(xc, 0).start()
+
+            return 0
+
+        lax.fori_loop(0, CHIPS, share_step, 0)
+
+        def sum_step(j, total):
+            xc = chip_at(j)
+            for i in (1, 3, 2):
+                q = col_at(i)
+                remote(
+                    s6.at[xc, q], r6.at[xc, q], send6.at[xc, i], recv6.at[xc, q],
+                    (s, pair, c),
+                ).wait_recv()
+                total = total + r6[xc, q].astype(f32)
+            return total
+
+        total = sum_step(0, after + s6[x_chip, c].astype(f32))
+
+        def far_step(j, total):
+            xc = chip_at(j)
             remote(
-                s6.at[row, q], r6.at[row, q], send6.at[other], recv6.at[other], (s, row, q)
+                s6.at[xc, c], r6.at[xc, c], send6.at[xc, 0], recv6.at[xc, c], (s, pair, c)
             ).wait_recv()
-            return total + r6[row, q].astype(f32)
-
-        total = lax.fori_loop(1, GROUP, sum_six, after + s6[r, c].astype(f32))
+            return sum_step(j, total + r6[xc, c].astype(f32))
+
+        total = lax.fori_loop(1, CHIPS, far_step, total)
         x_send[...] = total.astype(bf16)
 
         def send_one(i):
@@ -480,18 +530,18 @@
         for i in range(1, COLS):
             send_four(i).wait_send()
 
-        def finish(i, _):
-            other = lax.rem(me + i, GROUP)
-            row, q = other // COLS, lax.rem(other, COLS)
-            remote(
-                x2_all.at[r, c], x2_all.at[r, c], send5.at[i], recv5.at[me], (s, row, q)
-            ).wait_send()
-            remote(
-                s6.at[row, q], r6.at[r, c], send6.at[other], recv6.at[me], (s, row, q)
-            ).wait_send()
-            return 0
-
-        lax.fori_loop(1, GROUP, finish, 0)
+        for i in range(1, PEERS):
+            send_five(i).wait_send()
+        for i in range(CHIPS):
+            forward(i).wait_send()
+            swap(i).wait_send()
+            for k in range(1, COLS):
+                send_six(i, k).wait_send()
+
+            @pl.when(i != x_chip)
+            def _():
+                send_six(i, 0).wait_send()
+
         for i in range(COLS):
             send_one(i).wait_send()
         for i in range(COLS):
@@ -551,8 +601,11 @@
             pltpu.VMEM((COLS, SUB, WIDE), bf16),
             pltpu.VMEM((ROWS, COLS, SUB, WIDE), bf16),
             pltpu.VMEM((STREAMS, 2 * HIDDEN), f32),
-            pltpu.VMEM((ROWS, COLS, SUB, WIDE), bf16),
-            pltpu.VMEM((ROWS, COLS, SUB, WIDE), bf16),
+            pltpu.VMEM((CHIPS, STREAMS, WIDE), f32),
+            pltpu.VMEM((CHIPS, STREAMS, WIDE), bf16),
+            pltpu.VMEM((CHIPS, STREAMS, WIDE), bf16),
+            pltpu.VMEM((CHIPS, COLS, SUB, WIDE), bf16),
+            pltpu.VMEM((CHIPS, COLS, SUB, WIDE), bf16),
             pltpu.VMEM((SUB, WIDE), bf16),
             dma((7,)),
             dma((TURNS, 4)),
@@ -568,10 +621,14 @@
             dma((ROWS,)),
             dma((COLS,)),
             dma((COLS,)),
-            dma((GROUP,)),
-            dma((GROUP,)),
-            dma((GROUP,)),
-            dma((GROUP,)),
+            dma((PEERS,)),
+            dma((CHIPS, COLS)),
+            dma((CHIPS,)),
+            dma((CHIPS,)),
+            dma((CHIPS,)),
+            dma((CHIPS,)),
+            dma((CHIPS, COLS)),
+            dma((CHIPS, COLS)),
         ],
         compiler_params=pltpu.CompilerParams(
             collective_id=0, has_side_effects=True, vmem_limit_bytes=56 * 1024 * 1024

time: 181 us -> 158 us (0.87)
  Pallas kernels: 179 us -> 157 us
    pallas_call x1, Pallas kernels: 179 us -> 157 us  [per_device(): pl.pallas_call(kernel, out_shape=jax.ShapeDtypeStruct((1, STREAMS, PIECE)...]
where the time goes in v2:
time: 158 us
  Pallas kernels  157 us (99%)
    pallas_call x1, Pallas kernels, per_device(): pl.pallas_call(kernel, out_shape=jax.ShapeDtypeStruct((1, STREAMS, PIECE)...  157 us

profile of v2, /device:TPU:1, one launch (start us, length us, event | category | flops | bytes accessed | tf_op | source)
XLA Modules:
  0.0 158.2 jit_solution(17647533640475133744)
XLA Ops:
  0.0 156.8 %shard_map.127 = bf16[1,64,160]{2,1,0:T(8,128)(2,1)} custom-call(s32[4,8]{1,0:T(4,128)} %len_ref.1, bf16[1,64,160]{2,1,0:T(8,128)(2,1)} %hid_ref.1, bf16[1,160]{1,0:T(2,128)(2,1)} %ag_ref.1, bf16[1,160]{1,0:T(2,128)(2,1)} %fg_ref.1, bf16[1,640,1280]{2,1,0:T(8,128)(2,1)} %wq_hbm.1, bf16[1,640,256]{2,1,0:T(8,128)(2,1)} %wk_hbm.1, bf16[1,640,256]{2,1,0:T(8,128)(2,1)} %wv_hbm.1, ...), custom_call_target="tpu_custom_call" | custom-call | flops 5033164800 | bytes 24000000 | tf_op jit(solution)/shard_map/pallas_call | solution.py:580
  156.8 1.4 copy.15

commit v3 on v2

--- a/solution.py
+++ b/solution.py
@@ -21,8 +21,10 @@
 SUB = 16
 STREAMS = 64
 LOCAL = 8
-QKV = 1792
-HALF = 896
+KVSPLIT = 2
+QKV = 896
+PACK = 512
+OPACK = 384
 HIDDEN = 512
 norm_eps = 1e-06
 masked_score = -1e30
@@ -42,10 +44,10 @@
 
 
 def kernel(
-    len_ref,
-    hid_ref,
-    ag_ref,
-    fg_ref,
+    len_hbm,
+    hid_hbm,
+    ag_hbm,
+    fg_hbm,
     wq_hbm,
     wk_hbm,
     wv_hbm,
@@ -56,6 +58,10 @@
     kc_hbm,
     vc_hbm,
     out_ref,
+    len_ref,
+    hid_ref,
+    ag_ref,
+    fg_ref,
     wqkv,
     wo,
     wgu,
@@ -80,8 +86,10 @@
     s6,
     r6,
     x_send,
+    isem,
     wsem,
     csem,
+    zready,
     send0,
     recv0,
     sendg,
@@ -118,14 +126,27 @@
     def col_at(i):
         return lax.rem(c + i, COLS)
 
-    weight_copies = [
-        pltpu.make_async_copy(wq_hbm.at[0], wqkv.at[:, pl.ds(0, 1280)], wsem.at[0]),
-        pltpu.make_async_copy(wk_hbm.at[0], wqkv.at[:, pl.ds(1280, 256)], wsem.at[1]),
-        pltpu.make_async_copy(wv_hbm.at[0], wqkv.at[:, pl.ds(1536, 256)], wsem.at[2]),
-        pltpu.make_async_copy(wo_hbm.at[0], wo, wsem.at[3]),
-        pltpu.make_async_copy(wg_hbm.at[0], wgu.at[:, pl.ds(0, HIDDEN)], wsem.at[4]),
-        pltpu.make_async_copy(wu_hbm.at[0], wgu.at[:, pl.ds(HIDDEN, HIDDEN)], wsem.at[5]),
-        pltpu.make_async_copy(wd_hbm.at[0], wd, wsem.at[6]),
+    inputs = [
+        pltpu.make_async_copy(hid_hbm, hid_ref, isem.at[0]),
+        pltpu.make_async_copy(ag_hbm, ag_ref, isem.at[1]),
+        pltpu.make_async_copy(fg_hbm, fg_ref, isem.at[2]),
+        pltpu.make_async_copy(len_hbm, len_ref, isem.at[3]),
+    ]
+    weight_copies = []
+    for g in range(KVSPLIT):
+        for source, first, width in ((wq_hbm, 0, WIDE), (wk_hbm, WIDE, HD), (wv_hbm, WIDE + HD, HD)):
+            weight_copies.append(
+                pltpu.make_async_copy(
+                    source.at[0, :, pl.ds(g * width, width)],
+                    wqkv.at[:, pl.ds(g * QKV + first, width)],
+                    wsem.at[len(weight_copies)],
+                )
+            )
+    weight_copies += [
+        pltpu.make_async_copy(wo_hbm.at[0], wo, wsem.at[6]),
+        pltpu.make_async_copy(wg_hbm.at[0], wgu.at[:, pl.ds(0, HIDDEN)], wsem.at[7]),
+        pltpu.make_async_copy(wu_hbm.at[0], wgu.at[:, pl.ds(HIDDEN, HIDDEN)], wsem.at[8]),
+        pltpu.make_async_copy(wd_hbm.at[0], wd, wsem.at[9]),
     ]
 
     def cache_copies(t):
@@ -140,28 +161,29 @@
             )
         return copies
 
-    for copy in weight_copies[:3]:
+    barrier = pltpu.get_barrier_semaphore()
+    greeted = [(s, row_at(i), c) for i in range(1, ROWS)]
+    greeted += [(s, r, col_at(i)) for i in range(1, COLS)]
+    greeted += [(s_prev, r, c), (s_next, r, c)]
+    for device in greeted:
+        pl.semaphore_signal(
+            barrier, inc=1, device_id=device, device_id_type=pl.DeviceIdType.MESH
+        )
+
+    def row_of(dx):
+        return 2 * lax.rem(x_chip + dx, CHIPS) + core
+
+    for copy in inputs + weight_copies[:6]:
         copy.start()
     for copy in cache_copies(0):
         copy.start()
-    for copy in weight_copies[3:]:
+    for copy in weight_copies[6:]:
         copy.start()
     for t in range(1, TURNS):
         for copy in cache_copies(t):
             copy.start()
-
-    barrier = pltpu.get_barrier_semaphore()
-
-    def row_of(dx):
-        return 2 * lax.rem(x_chip + dx, CHIPS) + core
-
-    greeted = [(s, row_of(i // COLS), col_at(i % COLS)) for i in range(1, PEERS)]
-    greeted += [(s, 2 * lax.rem(x_chip + i, CHIPS) + 1 - core, c) for i in range(CHIPS)]
-    greeted += [(s_prev, r, i) for i in range(COLS)]
-    for device in greeted:
-        pl.semaphore_signal(
-            barrier, inc=1, device_id=device, device_id_type=pl.DeviceIdType.MESH
-        )
+    for copy in inputs:
+        copy.wait()
 
     init[c] = jnp.zeros((80, 256), bf16)
     init[c, 0:64, 0:PIECE] = hid_ref[0]
@@ -170,6 +192,21 @@
         gain_row == 0, ag_ref[...].astype(f32), fg_ref[...].astype(f32)
     ).astype(bf16)
 
+    pl.semaphore_wait(barrier, len(greeted))
+
+    def send_init(i):
+        return remote(
+            init.at[c], init.at[c], send0.at[i], recv0.at[c], (s, r, col_at(i))
+        )
+
+    def wait_init(i):
+        return remote(
+            init.at[col_at(i)], init.at[col_at(i)], send0.at[i], recv0.at[col_at(i)],
+            (s, r, col_at(i)),
+        )
+
+    for i in (2, 1, 3):
+        send_init(i).start()
     stream_row = lax.broadcasted_iota(jnp.int32, (LOCAL, LOCAL * CTX), 0)
     position = lax.broadcasted_iota(jnp.int32, (LOCAL, LOCAL * CTX), 1)
     for t in range(TURNS):
@@ -184,23 +221,11 @@
             offsets = jnp.where(live, 0.0, offsets)
         bias[t] = offsets
 
-    pl.semaphore_wait(barrier, len(greeted))
-
-    def send_init(i):
-        return remote(
-            init.at[c], init.at[c], send0.at[i], recv0.at[c], (s, r, col_at(i))
-        )
-
-    def wait_init(i):
-        return remote(
-            init.at[col_at(i)], init.at[col_at(i)], send0.at[i], recv0.at[col_at(i)],
-            (s, r, col_at(i)),
-        )
-
-    for i in range(1, COLS):
-        send_init(i).start()
     for i in range(1, COLS):
         wait_init(i).wait_recv()
+    pl.semaphore_signal(
+        zready, inc=1, device_id=(s_prev, r, c), device_id_type=pl.DeviceIdType.MESH
+    )
     joined = None
     for i in range(COLS):
         piece = jnp.concatenate(
@@ -233,54 +258,38 @@
 
         @pl.when(t == 0)
         def _():
-            for copy in weight_copies[:3]:
+            for copy in weight_copies[:6]:
                 copy.wait()
 
-        part = jnp.dot(left, wqkv[...], preferred_element_type=f32)
-        part = part.reshape(ROWS, LOCAL, QKV)
-        s2[:, :, 0:HALF] = jnp.concatenate(
-            [part[:, :, 0:HALF], part[:, :, HALF:QKV]], axis=1
-        ).astype(bf16)
-        s2[:, :, HALF:1024] = jnp.broadcast_to(
-            jnp.concatenate(
-                [high.reshape(ROWS, LOCAL, 1), low.reshape(ROWS, LOCAL, 1)], axis=1
-            ),
-            (ROWS, SUB, 128),
-        ).astype(bf16)
-
-        def send_two(i):
-            return remote(
-                s2.at[row_at(i)], r2.at[r], send2.at[i], recv2.at[r], (s, row_at(i), c)
-            )
-
-        def wait_two(i):
-            return remote(
-                s2.at[row_at(i)], r2.at[row_at(i)], send2.at[i], recv2.at[row_at(i)],
+        lane = lax.broadcasted_iota(jnp.int32, (STREAMS, 128), 1)
+        sums = jnp.where(lane < 64, high, low).reshape(ROWS, LOCAL, 128)
+
+        def send_two(g, i):
+            return remote(
+                s2.at[g, row_at(i)], r2.at[g, r], send2.at[g, i], recv2.at[g, r],
                 (s, row_at(i), c),
             )
 
-        for i in (4, 3, 5, 2, 6, 1, 7):
-            send_two(i).start()
+        def wait_two(g, i):
+            return remote(
+                s2.at[g, row_at(i)], r2.at[g, row_at(i)], send2.at[g, i],
+                recv2.at[g, row_at(i)], (s, row_at(i), c),
+            )
+
+        for g in range(KVSPLIT):
+            part = jnp.dot(
+                left, wqkv[:, g * QKV:(g + 1) * QKV], preferred_element_type=f32
+            ).reshape(ROWS, LOCAL, QKV)
+            rest = jnp.concatenate([part[:, :, PACK:QKV], sums], axis=2)
+            s2[g] = jnp.concatenate([part[:, :, 0:PACK], rest], axis=1).astype(bf16)
+            for i in (4, 3, 5, 2, 6, 1, 7):
+                send_two(g, i).start()
 
         @pl.when(t == 0)
         def _():
             for i in range(1, ROWS):
                 send_gain(i).start()
 
-        total = s2[r].astype(f32)
-        for i in (1, 7, 2, 6, 3, 5, 4):
-            wait_two(i).wait_recv()
-            total = total + r2[row_at(i)].astype(f32)
-        mean_square = (total[0:8, HALF:HALF + 1] + total[8:16, HALF:HALF + 1]) / D
-        scale = lax.rsqrt(mean_square + norm_eps)
-        top = (total[0:8, 0:HALF] * scale).astype(bf16).astype(f32)
-        bottom = (total[8:16, 0:HALF] * scale).astype(bf16).astype(f32)
-
-        def head(j):
-            if j < 7:
-                return top[:, j * HD:(j + 1) * HD]
-            return bottom[:, (j - 7) * HD:(j - 6) * HD]
-
         @pl.when(t == 0)
         def _():
             for copy in cache_copies(0):
@@ -291,13 +300,34 @@
             for copy in cache_copies(t):
                 copy.wait()
 
+        def send_three(g, i):
+            return remote(
+                o3.at[g, r], o3.at[g, r], send3.at[g, i], recv3.at[g, r], (s, row_at(i), c)
+            )
+
+        def wait_three(g, i):
+            return remote(
+                o3.at[g, row_at(i)], o3.at[g, row_at(i)], send3.at[g, i],
+                recv3.at[g, row_at(i)], (s, row_at(i), c),
+            )
+
         score_scale = 1.0 / math.sqrt(HD)
         offsets = jnp.concatenate([bias[t]] * 5, axis=0)
-        mixed_rows = []
-        for g in range(2):
-            queries = jnp.concatenate([head(5 * g + j) for j in range(5)], axis=0)
-            key_new = jnp.concatenate([head(10 + g)] * 5, axis=0)
-            value_new = jnp.concatenate([head(12 + g)] * 5, axis=0)
+        for g in range(KVSPLIT):
+            total = s2[g, r].astype(f32)
+            for i in (1, 7, 2, 6, 3, 5, 4):
+                wait_two(g, i).wait_recv()
+                total = total + r2[g, row_at(i)].astype(f32)
+            top, bottom = total[0:8], total[8:16]
+            mean_square = (bottom[:, 384:385] + bottom[:, 448:449]) / D
+            scale = lax.rsqrt(mean_square + norm_eps)
+            top = (top * scale).astype(bf16).astype(f32)
+            bottom = (bottom[:, 0:384] * scale).astype(bf16).astype(f32)
+            queries = jnp.concatenate(
+                [top[:, j * HD:(j + 1) * HD] for j in range(4)] + [bottom[:, 0:HD]], axis=0
+            )
+            key_new = jnp.concatenate([bottom[:, HD:2 * HD]] * 5, axis=0)
+            value_new = jnp.concatenate([bottom[:, 2 * HD:3 * HD]] * 5, axis=0)
             keys = kc[t, g].reshape(LOCAL * CTX, HD)
             values = vc[t, g].reshape(LOCAL * CTX, HD)
             scores = lax.dot_general(
@@ -314,37 +344,37 @@
             self_prob = (self_weight / denominator).astype(bf16).astype(f32)
             mixed = jnp.dot(probs, values, preferred_element_type=f32)
             mixed = mixed + self_prob * value_new
-            mixed_rows.append(
-                jnp.concatenate([mixed[j * 8:(j + 1) * 8] for j in range(5)], axis=1)
-            )
-        o3[r] = jnp.concatenate(mixed_rows, axis=0).astype(bf16)
-
-        def send_three(i):
-            return remote(
-                o3.at[r], o3.at[r], send3.at[i], recv3.at[r], (s, row_at(i), c)
-            )
-
-        def wait_three(i):
-            return remote(
-                o3.at[row_at(i)], o3.at[row_at(i)], send3.at[i], recv3.at[row_at(i)],
-                (s, row_at(i), c),
-            )
-
-        for i in (4, 3, 5, 2, 6, 1, 7):
-            send_three(i).start()
+            heads = [mixed[j * 8:(j + 1) * 8] for j in range(5)]
+            o3[g, r] = jnp.concatenate(
+                [
+                    jnp.concatenate(heads[0:3], axis=1),
+                    jnp.concatenate(heads[3:5] + [jnp.zeros((LOCAL, HD), f32)], axis=1),
+                ],
+                axis=0,
+            ).astype(bf16)
+            for i in (4, 3, 5, 2, 6, 1, 7):
+                send_three(g, i).start()
 
         @pl.when(t == 0)
         def _():
-            weight_copies[3].wait()
-
-        for i in (1, 7, 2, 6, 3, 5, 4):
-            wait_three(i).wait_recv()
-        gathered = o3[...].astype(f32)
-        heads = jnp.concatenate(
-            [gathered[:, 0:8].reshape(STREAMS, WIDE), gathered[:, 8:16].reshape(STREAMS, WIDE)],
-            axis=1,
-        ).astype(bf16)
-        out_part = jnp.dot(heads, wo[...], preferred_element_type=f32)
+            weight_copies[6].wait()
+
+        out_part = None
+        for g in range(KVSPLIT):
+            for i in (1, 7, 2, 6, 3, 5, 4):
+                wait_three(g, i).wait_recv()
+            gathered = o3[g].astype(f32)
+            heads = jnp.concatenate(
+                [
+                    gathered[:, 0:8].reshape(STREAMS, OPACK),
+                    gathered[:, 8:16, 0:WIDE - OPACK].reshape(STREAMS, WIDE - OPACK),
+                ],
+                axis=1,
+            ).astype(bf16)
+            product = jnp.dot(
+                heads, wo[g * WIDE:(g + 1) * WIDE, :], preferred_element_type=f32
+            )
+            out_part = product if out_part is None else out_part + product
         s4[...] = out_part.astype(bf16).reshape(COLS, SUB, WIDE)
 
         def send_four(i):
@@ -380,7 +410,7 @@
         def _():
             for i in range(1, ROWS):
                 wait_gain(i).wait_recv()
-            for copy in weight_copies[4:6]:
+            for copy in weight_copies[7:9]:
                 copy.wait()
 
         acc[...] = jnp.zeros_like(acc)
@@ -442,7 +472,7 @@
 
         @pl.when(t == 0)
         def _():
-            weight_copies[6].wait()
+            weight_copies[9].wait()
 
         def swap(xc):
             return remote(
@@ -521,12 +551,17 @@
                 (s_next, r, col_at(i)),
             )
 
-        for i in range(COLS):
+        @pl.when(t == 0)
+        def _():
+            pl.semaphore_wait(zready, 1)
+
+        for i in (2, 1, 3, 0):
             send_one(i).start()
 
-        for i in range(1, ROWS):
-            send_two(i).wait_send()
-            send_three(i).wait_send()
+        for g in range(KVSPLIT):
+            for i in range(1, ROWS):
+                send_two(g, i).wait_send()
+                send_three(g, i).wait_send()
         for i in range(1, COLS):
             send_four(i).wait_send()
 
@@ -580,10 +615,14 @@
     return pl.pallas_call(
         kernel,
         out_shape=jax.ShapeDtypeStruct((1, STREAMS, PIECE), bf16),
-        in_specs=[pl.BlockSpec(memory_space=pltpu.SMEM), vmem, vmem, vmem] + [hbm] * 9,
+        in_specs=[hbm] * 13,
         out_specs=vmem,
         scratch_shapes=[
-            pltpu.VMEM((WIDE, QKV), bf16),
+            pltpu.SMEM((TURNS, LOCAL), jnp.int32),
+            pltpu.VMEM((1, STREAMS, PIECE), bf16),
+            pltpu.VMEM((1, PIECE), bf16),
+            pltpu.VMEM((1, PIECE), bf16),
+            pltpu.VMEM((WIDE, KVSPLIT * QKV), bf16),
             pltpu.VMEM((1280, WIDE), bf16),
             pltpu.VMEM((D, 2 * HIDDEN), bf16),
             pltpu.VMEM((HIDDEN, D), bf16),
@@ -594,9 +633,9 @@
             pltpu.VMEM((ROWS, 8, WIDE), f32),
             pltpu.VMEM((TURNS, LOCAL, LOCAL * CTX), f32),
             pltpu.VMEM((TURNS + 1, COLS, SUB, WIDE), bf16),
-            pltpu.VMEM((ROWS, SUB, 1024), bf16),
-            pltpu.VMEM((ROWS, SUB, 1024), bf16),
-            pltpu.VMEM((ROWS, SUB, WIDE), bf16),
+            pltpu.VMEM((KVSPLIT, ROWS, SUB, PACK), bf16),
+            pltpu.VMEM((KVSPLIT, ROWS, SUB, PACK), bf16),
+            pltpu.VMEM((KVSPLIT, ROWS, SUB, OPACK), bf16),
             pltpu.VMEM((COLS, SUB, WIDE), bf16),
             pltpu.VMEM((COLS, SUB, WIDE), bf16),
             pltpu.VMEM((ROWS, COLS, SUB, WIDE), bf16),
@@ -607,18 +646,20 @@
             pltpu.VMEM((CHIPS, COLS, SUB, WIDE), bf16),
             pltpu.VMEM((CHIPS, COLS, SUB, WIDE), bf16),
             pltpu.VMEM((SUB, WIDE), bf16),
-            dma((7,)),
+            dma((4,)),
+            dma((10,)),
             dma((TURNS, 4)),
+            pltpu.SemaphoreType.REGULAR,
             dma((COLS,)),
             dma((COLS,)),
             dma((ROWS,)),
             dma((ROWS,)),
             dma((COLS,)),
             dma((TURNS, COLS)),
-            dma((ROWS,)),
-            dma((ROWS,)),
-            dma((ROWS,)),
-            dma((ROWS,)),
+            dma((KVSPLIT, ROWS)),
+            dma((KVSPLIT, ROWS)),
+            dma((KVSPLIT, ROWS)),
+            dma((KVSPLIT, ROWS)),
             dma((COLS,)),
             dma((COLS,)),
             dma((PEERS,)),

time: 158 us -> 156 us (0.987)
  Pallas kernels: 157 us -> 154 us
    pallas_call x1, Pallas kernels: 157 us -> 154 us  [per_device(): pl.pallas_call(kernel, out_shape=jax.ShapeDtypeStruct((1, STREAMS, PIECE)...]
where the time goes in v3:
time: 156 us
  Pallas kernels  154 us (99%)
    pallas_call x1, Pallas kernels, per_device(): pl.pallas_call(kernel, out_shape=jax.ShapeDtypeStruct((1, STREAMS, PIECE)...  154 us

profile of v3, /device:TPU:1, one launch (start us, length us, event | category | flops | bytes accessed | tf_op | source)
XLA Modules:
  0.0 155.8 jit_solution(8648872979990504239)
XLA Ops:
  0.0 154.4 %shard_map.127 = bf16[1,64,160]{2,1,0:T(8,128)(2,1)} custom-call(s32[4,8]{1,0:T(4,128)} %len_hbm.1, bf16[1,64,160]{2,1,0:T(8,128)(2,1)} %hid_hbm.1, bf16[1,160]{1,0:T(2,128)(2,1)} %ag_hbm.1, bf16[1,160]{1,0:T(2,128)(2,1)} %fg_hbm.1, bf16[1,640,1280]{2,1,0:T(8,128)(2,1)} %wq_hbm.1, bf16[1,640,256]{2,1,0:T(8,128)(2,1)} %wk_hbm.1, bf16[1,640,256]{2,1,0:T(8,128)(2,1)} %wv_hbm.1, ...), custom_call_target="tpu_custom_call" | custom-call | flops 5033164800 | bytes 24000000 | tf_op jit(solution)/shard_map/pallas_call | solution.py:615
  154.4 1.4 copy.15

commit v4 on v3

--- a/solution.py
+++ b/solution.py
@@ -80,9 +80,8 @@
     r4,
     x2_all,
     acc,
-    keep,
-    p6,
-    q6,
+    mine,
+    theirs,
     s6,
     r6,
     x_send,
@@ -104,10 +103,10 @@
     recv4,
     send5,
     recv5,
-    send_f,
-    recv_f,
     send_p,
     recv_p,
+    send_w,
+    recv_w,
     send6,
     recv6,
 ):
@@ -144,10 +143,46 @@
             )
     weight_copies += [
         pltpu.make_async_copy(wo_hbm.at[0], wo, wsem.at[6]),
-        pltpu.make_async_copy(wg_hbm.at[0], wgu.at[:, pl.ds(0, HIDDEN)], wsem.at[7]),
-        pltpu.make_async_copy(wu_hbm.at[0], wgu.at[:, pl.ds(HIDDEN, HIDDEN)], wsem.at[8]),
-        pltpu.make_async_copy(wd_hbm.at[0], wd, wsem.at[9]),
+        pltpu.make_async_copy(
+            wg_hbm.at[:, core], wgu.at[core, :, :, pl.ds(0, HIDDEN)], wsem.at[7]
+        ),
+        pltpu.make_async_copy(
+            wu_hbm.at[:, core], wgu.at[core, :, :, pl.ds(HIDDEN, HIDDEN)], wsem.at[8]
+        ),
     ]
+    other_copies = [
+        remote(
+            wg_hbm.at[:, 1 - core], wgu.at[core, :, :, pl.ds(0, HIDDEN)],
+            send_w.at[0], recv_w.at[0], (s, pair, c),
+        ),
+        remote(
+            wu_hbm.at[:, 1 - core], wgu.at[core, :, :, pl.ds(HIDDEN, HIDDEN)],
+            send_w.at[1], recv_w.at[1], (s, pair, c),
+        ),
+    ]
+    for i in range(CHIPS):
+        ours = pl.multiple_of((2 * i + core) * WIDE, WIDE)
+        other = pl.multiple_of((2 * i + 1 - core) * WIDE, WIDE)
+        weight_copies.append(
+            pltpu.make_async_copy(
+                wd_hbm.at[0, :, pl.ds(ours, WIDE)],
+                wd.at[core, :, pl.ds(i * WIDE, WIDE)],
+                wsem.at[9 + i],
+            )
+        )
+        other_copies.append(
+            remote(
+                wd_hbm.at[0, :, pl.ds(other, WIDE)], wd.at[core, :, pl.ds(i * WIDE, WIDE)],
+                send_w.at[2 + i], recv_w.at[2 + i], (s, pair, c),
+            )
+        )
+
+    def wait_other(i):
+        if i < 2:
+            place = wgu.at[1 - core, :, :, pl.ds(i * HIDDEN, HIDDEN)]
+        else:
+            place = wd.at[1 - core, :, pl.ds((i - 2) * WIDE, WIDE)]
+        remote(place, place, send_w.at[i], recv_w.at[i], (s, pair, c)).wait_recv()
 
     def cache_copies(t):
         m = lax.rem(s + TURNS - t, TURNS)
@@ -207,6 +242,8 @@
 
     for i in (2, 1, 3):
         send_init(i).start()
+    for copy in other_copies[:1]:
+        copy.start()
     stream_row = lax.broadcasted_iota(jnp.int32, (LOCAL, LOCAL * CTX), 0)
     position = lax.broadcasted_iota(jnp.int32, (LOCAL, LOCAL * CTX), 1)
     for t in range(TURNS):
@@ -287,8 +324,9 @@
 
         @pl.when(t == 0)
         def _():
-            for i in range(1, ROWS):
+            for i in (2, 4, 6):
                 send_gain(i).start()
+            other_copies[1].start()
 
         @pl.when(t == 0)
         def _():
@@ -358,6 +396,8 @@
         @pl.when(t == 0)
         def _():
             weight_copies[6].wait()
+            for copy in other_copies[2:]:
+                copy.start()
 
         out_part = None
         for g in range(KVSPLIT):
@@ -394,12 +434,12 @@
         for i in (1, 3, 2):
             wait_four(i).wait_recv()
             after = after + r4[col_at(i)].astype(f32)
-        x2_all[r, c] = after.astype(bf16)
-        after = x2_all[r, c].astype(f32)
+        x2_all[x_chip, c] = after.astype(bf16)
+        after = x2_all[x_chip, c].astype(f32)
 
         def send_five(i):
             return remote(
-                x2_all.at[r, c], x2_all.at[r, c], send5.at[i], recv5.at[x_chip, c],
+                x2_all.at[x_chip, c], x2_all.at[x_chip, c], send5.at[i], recv5.at[x_chip, c],
                 (s, row_of(i // COLS), col_at(i % COLS)),
             )
 
@@ -408,103 +448,94 @@
 
         @pl.when(t == 0)
         def _():
-            for i in range(1, ROWS):
+            for i in (2, 4, 6):
                 wait_gain(i).wait_recv()
             for copy in weight_copies[7:9]:
                 copy.wait()
-
-        acc[...] = jnp.zeros_like(acc)
+            for i in range(2):
+                wait_other(i)
 
         def chip_at(j):
             return lax.rem(x_chip + j + (j // 2) * (5 - 2 * j), 4)
 
-        def forward(xc):
-            row = 2 * xc + core
-            return remote(
-                x2_all.at[row], x2_all.at[row], send_f.at[xc], recv_f.at[xc], (s, pair, c)
-            )
-
-        def collect(j):
+        def collect(xc, own):
+            for i in (1, 3, 2) if own else (1, 3, 2, 0):
+                q = col_at(i)
+                remote(
+                    x2_all.at[xc, q], x2_all.at[xc, q], send5.at[1], recv5.at[xc, q],
+                    (s, pair, c),
+                ).wait_recv()
+            values = x2_all[xc].reshape(STREAMS, WIDE).astype(f32)
+            square = values * values
+            squares = square[:, 0:128]
+            for k in range(1, 5):
+                squares = squares + square[:, k * 128:(k + 1) * 128]
+            return (values * gain2[2 * xc + core, 0:1]).astype(bf16), squares
+
+        def gate_part(scaled, xc, h):
+            return jnp.dot(scaled, wgu[h, xc], preferred_element_type=f32)
+
+        scaled, squares = collect(x_chip, True)
+        for h in range(2):
+            acc[h] = gate_part(scaled, x_chip, h)
+
+        def gate_step(j, squares):
             xc = chip_at(j)
-            for q in range(COLS):
-
-                @pl.when((xc != x_chip) | (q != c))
-                def _():
-                    row = 2 * xc + core
-                    remote(
-                        x2_all.at[row, q], x2_all.at[row, q], send5.at[0],
-                        recv5.at[xc, q], (s, pair, c),
-                    ).wait_recv()
-
-            forward(xc).start()
-
-        def gate_step(j, squares):
-            @pl.when(j < CHIPS - 1)
-            def _():
-                collect(j + 1)
-
-            xc = chip_at(j)
-            row = 2 * xc + 1 - core
-            remote(
-                x2_all.at[row], x2_all.at[row], send_f.at[xc], recv_f.at[xc], (s, pair, c)
-            ).wait_recv()
-            values = jnp.concatenate(
-                [x2_all[2 * xc + k].reshape(STREAMS, WIDE) for k in range(2)], axis=1
-            ).astype(f32)
-            gains = jnp.concatenate([gain2[2 * xc + k, 0:1] for k in range(2)], axis=1)
-            square = values * values
-            for k in range(10):
-                squares = squares + square[:, k * 128:(k + 1) * 128]
-            scaled = (values * gains).astype(bf16)
-            first = pl.multiple_of(xc * 1280, 1280)
-            acc[...] += jnp.dot(
-                scaled, wgu[pl.ds(first, 1280), :], preferred_element_type=f32
-            )
-            return squares
-
-        collect(0)
-        squares = lax.fori_loop(0, CHIPS, gate_step, jnp.zeros((STREAMS, 128), f32))
-        mean_square = jnp.sum(squares, axis=1, keepdims=True) / D
-        scale = lax.rsqrt(mean_square + norm_eps)
-        gate = acc[:, 0:HIDDEN] * scale
-        up = acc[:, HIDDEN:2 * HIDDEN] * scale
-        activation = (gate / (1.0 + jnp.exp(-gate)) * up).astype(bf16)
+            scaled, more = collect(xc, False)
+            for h in range(2):
+                acc[h] += gate_part(scaled, xc, h)
+            return squares + more
+
+        squares = lax.fori_loop(1, CHIPS - 1, gate_step, squares)
+
+        def swap(h):
+            return remote(
+                mine.at[h], theirs.at[h], send_p.at[h], recv_p.at[h], (s, pair, c)
+            )
+
+        far = chip_at(CHIPS - 1)
+        scaled, more = collect(far, False)
+        squares = jnp.sum(squares + more, axis=1, keepdims=True)
+        high = squares.astype(bf16).astype(f32)
+        sums = jnp.where(lane < 64, high, squares - high)
+        for h in range(2):
+            product = acc[h] + gate_part(scaled, far, h)
+            acc[h] = product
+            mine[h] = jnp.concatenate([product, sums], axis=1).astype(bf16)
+            swap(h).start()
+        activations = []
+        for h in range(2):
+            swap(h).wait_recv()
+            other = theirs[h].astype(f32)
+            if h == 0:
+                tail = other[:, 1024:1152]
+                mean_square = (squares + tail[:, 0:1] + tail[:, 64:65]) / D
+                scale = lax.rsqrt(mean_square + norm_eps)
+            both = (acc[h] + other[:, 0:1024]) * scale
+            gate, up = both[:, 0:HIDDEN], both[:, HIDDEN:2 * HIDDEN]
+            activations.append((gate / (1.0 + jnp.exp(-gate)) * up).astype(bf16))
+        activation = jnp.concatenate(activations, axis=1)
 
         @pl.when(t == 0)
         def _():
-            weight_copies[9].wait()
-
-        def swap(xc):
-            return remote(
-                p6.at[xc], q6.at[xc], send_p.at[xc], recv_p.at[xc], (s, pair, c)
+            for copy in weight_copies[9:13]:
+                copy.wait()
+            for i in range(2, 6):
+                wait_other(i)
+
+        def send_six(xc, i):
+            q = col_at(i)
+            return remote(
+                s6.at[xc, q], r6.at[x_chip, c], send6.at[xc, i], recv6.at[x_chip, c],
+                (s, 2 * xc + core, q),
             )
 
         def down_step(j, _):
             xc = chip_at(CHIPS - 1 - j)
-            first = pl.multiple_of(xc * 1280, 1280)
-            part = jnp.dot(
-                activation, wd[:, pl.ds(first, 1280)], preferred_element_type=f32
-            )
-            lower, upper = part[:, 0:WIDE], part[:, WIDE:1280]
-            keep[xc] = jnp.where(core == 0, lower, upper)
-            p6[xc] = jnp.where(core == 0, upper, lower).astype(bf16)
-            swap(xc).start()
-            return 0
-
-        lax.fori_loop(0, CHIPS, down_step, 0)
-
-        def send_six(xc, i):
-            q = col_at(i)
-            return remote(
-                s6.at[xc, q], r6.at[x_chip, c], send6.at[xc, i], recv6.at[x_chip, c],
-                (s, 2 * xc + core, q),
-            )
-
-        def share_step(j, _):
-            xc = chip_at(CHIPS - 1 - j)
-            swap(xc).wait_recv()
-            both = keep[xc] + q6[xc].astype(f32)
-            s6[xc] = both.astype(bf16).reshape(COLS, SUB, WIDE)
+            first = pl.multiple_of(xc * WIDE, WIDE)
+            columns = wd[:, :, pl.ds(first, WIDE)].reshape(2 * HIDDEN, WIDE)
+            part = jnp.dot(activation, columns, preferred_element_type=f32)
+            s6[xc] = part.astype(bf16).reshape(COLS, SUB, WIDE)
             for i in (2, 1, 3):
                 send_six(xc, i).start()
 
@@ -514,7 +545,7 @@
 
             return 0
 
-        lax.fori_loop(0, CHIPS, share_step, 0)
+        lax.fori_loop(0, CHIPS, down_step, 0)
 
         def sum_step(j, total):
             xc = chip_at(j)
@@ -567,9 +598,9 @@
 
         for i in range(1, PEERS):
             send_five(i).wait_send()
+        for h in range(2):
+            swap(h).wait_send()
         for i in range(CHIPS):
-            forward(i).wait_send()
-            swap(i).wait_send()
             for k in range(1, COLS):
                 send_six(i, k).wait_send()
 
@@ -590,8 +621,10 @@
     out_ref[0] = final[:, 0:PIECE].astype(bf16)
     for i in range(1, COLS):
         send_init(i).wait_send()
-    for i in range(1, ROWS):
+    for i in (2, 4, 6):
         send_gain(i).wait_send()
+    for copy in other_copies:
+        copy.wait_send()
 
 
 def per_device(
@@ -624,8 +657,8 @@
             pltpu.VMEM((1, PIECE), bf16),
             pltpu.VMEM((WIDE, KVSPLIT * QKV), bf16),
             pltpu.VMEM((1280, WIDE), bf16),
-            pltpu.VMEM((D, 2 * HIDDEN), bf16),
-            pltpu.VMEM((HIDDEN, D), bf16),
+            pltpu.VMEM((2, CHIPS, WIDE, 2 * HIDDEN), bf16),
+            pltpu.VMEM((2, HIDDEN, CHIPS * WIDE), bf16),
             pltpu.VMEM((TURNS, 2, LOCAL, CTX, HD), bf16),
             pltpu.VMEM((TURNS, 2, LOCAL, CTX, HD), bf16),
             pltpu.VMEM((COLS, 80, 256), bf16),
@@ -638,16 +671,15 @@
             pltpu.VMEM((KVSPLIT, ROWS, SUB, OPACK), bf16),
             pltpu.VMEM((COLS, SUB, WIDE), bf16),
             pltpu.VMEM((COLS, SUB, WIDE), bf16),
-            pltpu.VMEM((ROWS, COLS, SUB, WIDE), bf16),
-            pltpu.VMEM((STREAMS, 2 * HIDDEN), f32),
-            pltpu.VMEM((CHIPS, STREAMS, WIDE), f32),
-            pltpu.VMEM((CHIPS, STREAMS, WIDE), bf16),
-            pltpu.VMEM((CHIPS, STREAMS, WIDE), bf16),
+            pltpu.VMEM((CHIPS, COLS, SUB, WIDE), bf16),
+            pltpu.VMEM((2, STREAMS, 2 * HIDDEN), f32),
+            pltpu.VMEM((2, STREAMS, 2 * HIDDEN + 128), bf16),
+            pltpu.VMEM((2, STREAMS, 2 * HIDDEN + 128), bf16),
             pltpu.VMEM((CHIPS, COLS, SUB, WIDE), bf16),
             pltpu.VMEM((CHIPS, COLS, SUB, WIDE), bf16),
             pltpu.VMEM((SUB, WIDE), bf16),
             dma((4,)),
-            dma((10,)),
+            dma((13,)),
             dma((TURNS, 4)),
             pltpu.SemaphoreType.REGULAR,
             dma((COLS,)),
@@ -664,10 +696,10 @@
             dma((COLS,)),
             dma((PEERS,)),
             dma((CHIPS, COLS)),
-            dma((CHIPS,)),
-            dma((CHIPS,)),
-            dma((CHIPS,)),
-            dma((CHIPS,)),
+            dma((2,)),
+            dma((2,)),
+            dma((6,)),
+            dma((6,)),
             dma((CHIPS, COLS)),
             dma((CHIPS, COLS)),
         ],
@@ -686,8 +718,8 @@
         key_weight,
         value_weight,
         out_weight,
-        gate_weight,
-        up_weight,
+        gate_weight.reshape(CHIPS, 2, WIDE, HIDDEN),
+        up_weight.reshape(CHIPS, 2, WIDE, HIDDEN),
         down_weight,
         key_cache,
         value_cache,

time: 156 us -> 148 us (0.949)
  Pallas kernels: 154 us -> 147 us
    pallas_call x1, Pallas kernels: 154 us -> 147 us  [per_device(): pl.pallas_call(kernel, out_shape=jax.ShapeDtypeStruct((1, STREAMS, PIECE)...]
where the time goes in v4:
time: 148 us
  Pallas kernels  147 us (99%)
    pallas_call x1, Pallas kernels, per_device(): pl.pallas_call(kernel, out_shape=jax.ShapeDtypeStruct((1, STREAMS, PIECE)...  147 us

profile of v4, /device:TPU:1, one launch (start us, length us, event | category | flops | bytes accessed | tf_op | source)
XLA Modules:
  0.0 148.1 jit_solution(17619939966930451148)
XLA Ops:
  0.0 146.7 %shard_map.127 = bf16[1,64,160]{2,1,0:T(8,128)(2,1)} custom-call(s32[4,8]{1,0:T(4,128)} %len_hbm.1, bf16[1,64,160]{2,1,0:T(8,128)(2,1)} %hid_hbm.1, bf16[1,160]{1,0:T(2,128)(2,1)} %ag_hbm.1, bf16[1,160]{1,0:T(2,128)(2,1)} %fg_hbm.1, bf16[1,640,1280]{2,1,0:T(8,128)(2,1)} %wq_hbm.1, bf16[1,640,256]{2,1,0:T(8,128)(2,1)} %wk_hbm.1, bf16[1,640,256]{2,1,0:T(8,128)(2,1)} %wv_hbm.1, ...), custom_call_target="tpu_custom_call" | custom-call | flops 5033164800 | bytes 24000000 | tf_op jit(solution)/shard_map/pallas_call | solution.py:648
  146.7 1.4 copy.15

commit v5 on v4

--- a/solution.py
+++ b/solution.py
@@ -378,8 +378,9 @@
             weights = jnp.exp(scores - row_max)
             self_weight = jnp.exp(self_score - row_max)
             denominator = jnp.sum(weights, axis=1, keepdims=True) + self_weight
-            probs = (weights / denominator).astype(bf16)
-            self_prob = (self_weight / denominator).astype(bf16).astype(f32)
+            share = 1.0 / denominator
+            probs = (weights * share).astype(bf16)
+            self_prob = (self_weight * share).astype(bf16).astype(f32)
             mixed = jnp.dot(probs, values, preferred_element_type=f32)
             mixed = mixed + self_prob * value_new
             heads = [mixed[j * 8:(j + 1) * 8] for j in range(5)]
@@ -503,6 +504,16 @@
             acc[h] = product
             mine[h] = jnp.concatenate([product, sums], axis=1).astype(bf16)
             swap(h).start()
+        @pl.when(t == 0)
+        def _():
+            for copy in weight_copies[9:13]:
+                copy.wait()
+            for i in range(2, 6):
+                wait_other(i)
+
+        def down_columns(xc):
+            return pl.ds(pl.multiple_of(xc * WIDE, WIDE), WIDE)
+
         activations = []
         for h in range(2):
             swap(h).wait_recv()
@@ -513,15 +524,13 @@
                 scale = lax.rsqrt(mean_square + norm_eps)
             both = (acc[h] + other[:, 0:1024]) * scale
             gate, up = both[:, 0:HIDDEN], both[:, HIDDEN:2 * HIDDEN]
-            activations.append((gate / (1.0 + jnp.exp(-gate)) * up).astype(bf16))
+            half = 0.5 * gate
+            activations.append(((half + half * jnp.tanh(half)) * up).astype(bf16))
+            if h == 0:
+                far_part = jnp.dot(
+                    activations[0], wd[0, :, down_columns(far)], preferred_element_type=f32
+                )
         activation = jnp.concatenate(activations, axis=1)
-
-        @pl.when(t == 0)
-        def _():
-            for copy in weight_copies[9:13]:
-                copy.wait()
-            for i in range(2, 6):
-                wait_other(i)
 
         def send_six(xc, i):
             q = col_at(i)
@@ -530,11 +539,7 @@
                 (s, 2 * xc + core, q),
             )
 
-        def down_step(j, _):
-            xc = chip_at(CHIPS - 1 - j)
-            first = pl.multiple_of(xc * WIDE, WIDE)
-            columns = wd[:, :, pl.ds(first, WIDE)].reshape(2 * HIDDEN, WIDE)
-            part = jnp.dot(activation, columns, preferred_element_type=f32)
+        def send_part(xc, part):
             s6[xc] = part.astype(bf16).reshape(COLS, SUB, WIDE)
             for i in (2, 1, 3):
                 send_six(xc, i).start()
@@ -543,9 +548,17 @@
             def _():
                 send_six(xc, 0).start()
 
+        def down_step(j, _):
+            xc = lax.rem(x_chip + lax.rem(2 * j + 2, 4) + j // 2, CHIPS)
+            columns = wd[:, :, down_columns(xc)].reshape(2 * HIDDEN, WIDE)
+            send_part(xc, jnp.dot(activation, columns, preferred_element_type=f32))
             return 0
 
-        lax.fori_loop(0, CHIPS, down_step, 0)
+        far_part = far_part + jnp.dot(
+            activations[1], wd[1, :, down_columns(far)], preferred_element_type=f32
+        )
+        send_part(far, far_part)
+        lax.fori_loop(1, CHIPS, down_step, 0)
 
         def sum_step(j, total):
             xc = chip_at(j)

time: 148 us -> 146 us (0.986)
  Pallas kernels: 147 us -> 144 us
    pallas_call x1, Pallas kernels: 147 us -> 144 us  [per_device(): pl.pallas_call(kernel, out_shape=jax.ShapeDtypeStruct((1, STREAMS, PIECE)...]
where the time goes in v5:
time: 146 us
  Pallas kernels  144 us (99%)
    pallas_call x1, Pallas kernels, per_device(): pl.pallas_call(kernel, out_shape=jax.ShapeDtypeStruct((1, STREAMS, PIECE)...  144 us

profile of v5, /device:TPU:1, one launch (start us, length us, event | category | flops | bytes accessed | tf_op | source)
XLA Modules:
  0.0 145.8 jit_solution(10826772379517955346)
XLA Ops:
  0.0 144.4 %shard_map.127 = bf16[1,64,160]{2,1,0:T(8,128)(2,1)} custom-call(s32[4,8]{1,0:T(4,128)} %len_hbm.1, bf16[1,64,160]{2,1,0:T(8,128)(2,1)} %hid_hbm.1, bf16[1,160]{1,0:T(2,128)(2,1)} %ag_hbm.1, bf16[1,160]{1,0:T(2,128)(2,1)} %fg_hbm.1, bf16[1,640,1280]{2,1,0:T(8,128)(2,1)} %wq_hbm.1, bf16[1,640,256]{2,1,0:T(8,128)(2,1)} %wk_hbm.1, bf16[1,640,256]{2,1,0:T(8,128)(2,1)} %wv_hbm.1, ...), custom_call_target="tpu_custom_call" | custom-call | flops 5033164800 | bytes 24000000 | tf_op jit(solution)/shard_map/pallas_call | solution.py:661
  144.4 1.4 copy.15

commit v6 on v5

--- a/solution.py
+++ b/solution.py
@@ -660,7 +660,7 @@
     dma = pltpu.SemaphoreType.DMA
     return pl.pallas_call(
         kernel,
-        out_shape=jax.ShapeDtypeStruct((1, STREAMS, PIECE), bf16),
+        out_shape=pltpu.VMEM((1, STREAMS, PIECE), bf16),
         in_specs=[hbm] * 13,
         out_specs=vmem,
         scratch_shapes=[

time: 146 us -> 145 us (level)
  no operation moved by 1% of the time
where the time goes in v6:
time: 145 us
  Pallas kernels  144 us (99%)
    pallas_call x1, Pallas kernels, per_device(): pl.pallas_call(kernel, out_shape=pltpu.VMEM((1, STREAMS, PIECE), bf16), i...  144 us

profile of v6, /device:TPU:1, one launch (start us, length us, event | category | flops | bytes accessed | tf_op | source)
XLA Modules:
  0.0 144.8 jit_solution(18314468316705549004)
XLA Ops:
  0.0 144.2 %shard_map.127 = bf16[1,64,160]{2,1,0:T(8,128)(2,1)S(1)} custom-call(s32[4,8]{1,0:T(4,128)} %len_hbm.1, bf16[1,64,160]{2,1,0:T(8,128)(2,1)} %hid_hbm.1, bf16[1,160]{1,0:T(2,128)(2,1)} %ag_hbm.1, bf16[1,160]{1,0:T(2,128)(2,1)} %fg_hbm.1, bf16[1,640,1280]{2,1,0:T(8,128)(2,1)} %wq_hbm.1, bf16[1,640,256]{2,1,0:T(8,128)(2,1)} %wk_hbm.1, ...), custom_call_target="tpu_custom_call" | custom-call | flops 5033164800 | bytes 24000000 | tf_op jit(solution)/shard_map/pallas_call | solution.py:661
  144.2 0.6 copy.15

commit v7 on v6

--- a/solution.py
+++ b/solution.py
@@ -68,6 +68,7 @@
     wd,
     kc,
     vc,
+    stage,
     init,
     gain1,
     gain2,
@@ -220,12 +221,19 @@
     for copy in inputs:
         copy.wait()
 
-    init[c] = jnp.zeros((80, 256), bf16)
-    init[c, 0:64, 0:PIECE] = hid_ref[0]
+    stage[...] = jnp.zeros((80, 256), bf16)
+    stage[0:64, 0:PIECE] = hid_ref[0]
     gain_row = lax.broadcasted_iota(jnp.int32, (SUB, PIECE), 0)
-    init[c, 64:80, 0:PIECE] = jnp.where(
+    stage[64:80, 0:PIECE] = jnp.where(
         gain_row == 0, ag_ref[...].astype(f32), fg_ref[...].astype(f32)
     ).astype(bf16)
+
+    ends = stage[:, 128:256].astype(f32)
+    packed = ends[0:16]
+    for i in range(1, 4):
+        packed = packed + pltpu.roll(ends[16 * i:16 * i + 16], 32 * i, 1)
+    init[c, 0:80] = stage[:, 0:128]
+    init[c, 80:112] = jnp.concatenate([packed, ends[64:80]], axis=0).astype(bf16)
 
     pl.semaphore_wait(barrier, len(greeted))
 
@@ -265,8 +273,17 @@
     )
     joined = None
     for i in range(COLS):
+        message = init[i].astype(f32)
+        packed = message[80:96]
+        ends = jnp.concatenate(
+            [packed] + [pltpu.roll(packed, 128 - 32 * k, 1) for k in range(1, 4)]
+            + [message[96:112]],
+            axis=0,
+        )
+        end_lane = lax.broadcasted_iota(jnp.int32, (80, 128), 1)
+        ends = jnp.where(end_lane < PIECE - 128, ends, 0.0)
         piece = jnp.concatenate(
-            [init[i].astype(f32), jnp.zeros((80, WIDE - 256), f32)], axis=1
+            [message[0:80], ends, jnp.zeros((80, WIDE - 256), f32)], axis=1
         )
         if i:
             piece = pltpu.roll(piece, i * PIECE, 1)
@@ -674,7 +691,8 @@
             pltpu.VMEM((2, HIDDEN, CHIPS * WIDE), bf16),
             pltpu.VMEM((TURNS, 2, LOCAL, CTX, HD), bf16),
             pltpu.VMEM((TURNS, 2, LOCAL, CTX, HD), bf16),
-            pltpu.VMEM((COLS, 80, 256), bf16),
+            pltpu.VMEM((80, 256), bf16),
+            pltpu.VMEM((COLS, 112, 128), bf16),
             pltpu.VMEM((1, WIDE), f32),
             pltpu.VMEM((ROWS, 8, WIDE), f32),
             pltpu.VMEM((TURNS, LOCAL, LOCAL * CTX), f32),

time: 145 us -> 145 us (level)
  no operation moved by 1% of the time
where the time goes in v7:
time: 145 us
  Pallas kernels  144 us (99%)
    pallas_call x1, Pallas kernels, per_device(): pl.pallas_call(kernel, out_shape=pltpu.VMEM((1, STREAMS, PIECE), bf16), i...  144 us

profile of v7, /device:TPU:1, one launch (start us, length us, event | category | flops | bytes accessed | tf_op | source)
XLA Modules:
  0.0 144.7 jit_solution(10729038111789060552)
XLA Ops:
  0.0 144.1 %shard_map.127 = bf16[1,64,160]{2,1,0:T(8,128)(2,1)S(1)} custom-call(s32[4,8]{1,0:T(4,128)} %len_hbm.1, bf16[1,64,160]{2,1,0:T(8,128)(2,1)} %hid_hbm.1, bf16[1,160]{1,0:T(2,128)(2,1)} %ag_hbm.1, bf16[1,160]{1,0:T(2,128)(2,1)} %fg_hbm.1, bf16[1,640,1280]{2,1,0:T(8,128)(2,1)} %wq_hbm.1, bf16[1,640,256]{2,1,0:T(8,128)(2,1)} %wk_hbm.1, ...), custom_call_target="tpu_custom_call" | custom-call | flops 5033164800 | bytes 24000000 | tf_op jit(solution)/shard_map/pallas_call | solution.py:678
  144.1 0.6 copy.15
